TPU v7x, 256 devices: a whole 4x4x8 slice. The times are simulated.
256 devices in a mesh: dp: 32 (over z, x), expert: 8 (over y, core).
Axes of the slice: x: 4, y: 4, z: 8, core: 2. Of those that a mesh axis runs over, the one named last changes fastest.
Arguments:
- out_grad: bfloat16 [1024, 3072], P('expert'), may hold values from -1.1953125 to 1.1953125
- routes: int32 [1024, 4], P('expert'), may hold values from 0 to 7, all different within a row; in each aligned block of 128 rows (0 to 127, 128 to 255, ...) at most 80 rows name the same one
- gate_values: float32 [1024, 4], P('expert'), may hold values from 0.1 to 0.5
- layer_input: bfloat16 [1024, 3072], P('expert'), may hold values from -6 to 6
- w_gate: bfloat16 [8, 3072, 8192], P('expert', None, 'dp'), may hold values from -0.109375 to 0.109375
- w_up: bfloat16 [8, 3072, 8192], P('expert', None, 'dp'), may hold values from -0.109375 to 0.109375
- w_down: bfloat16 [8, 3072, 8192], P('expert', None, 'dp'), may hold values from -0.109375 to 0.109375
Outputs:
- input_grad: bfloat16 [1024, 3072], P('expert')
- grad_gate: float32 [8, 3072, 8192], P('expert', None, 'dp')
- grad_up: float32 [8, 3072, 8192], P('expert', None, 'dp')
Inputs may be any that keep to these rules, and one draw needn't show every extreme that they name: In every aligned block of 128 tokens (the tokens of one index of expert) no expert is named by more than 80 routes, a bound that some block reaches; the 4 experts of a token differ.
All inputs are finite; a program needn't handle non-finite values.
Results may differ from a plain program's by a relative error of at most 0.024.
Values may be sent and summed in bfloat16 or wider, within the bound.
A program may use at most 128 MiB of HBM per device.

v0:
```python
import jax
import jax.numpy as jnp
from jax import lax
from jax.sharding import PartitionSpec as P

EXPERTS = 8
MOST = 80


def local(out_grad, routes, gate_values, layer_input, w_gate, w_up, w_down):
    expert_count = lax.axis_size("expert")
    tok_dev, features = out_grad.shape
    per_token = routes.shape[1]
    exp_dev = w_gate.shape[0]
    local_units = w_gate.shape[2]
    capacity = MOST
    flat_routes = routes.reshape(-1)
    experts_row = jnp.arange(EXPERTS, dtype=jnp.int32)[None, :]
    onehot = (flat_routes[:, None] == experts_row).astype(jnp.int32)
    slot_index = jnp.sum((jnp.cumsum(onehot, axis=0) - onehot) * onehot, axis=1)
    target = flat_routes * capacity + slot_index
    scaled = gate_values[:, :, None] * out_grad[:, None, :].astype(jnp.float32)
    scaled = scaled.reshape(tok_dev * per_token, features).astype(jnp.bfloat16)
    copies = jnp.broadcast_to(layer_input[:, None, :], (tok_dev, per_token, features)).reshape(
        -1, features
    )
    blank_slots = jnp.zeros((EXPERTS * capacity, features), jnp.bfloat16)
    rows_out = blank_slots.at[target].set(copies).reshape(expert_count, exp_dev, capacity, features)
    grads_out = (
        blank_slots.at[target].set(scaled).reshape(expert_count, exp_dev, capacity, features)
    )
    rows_in, grads_in = (
        lax.all_to_all(rows_out, "expert", split_axis=0, concat_axis=0, tiled=True),
        lax.all_to_all(grads_out, "expert", split_axis=0, concat_axis=0, tiled=True),
    )
    gate_pre = jnp.einsum("slja,laf->jslf", rows_in, w_gate, preferred_element_type=jnp.float32)
    up_pre = jnp.einsum("slja,laf->jslf", rows_in, w_up, preferred_element_type=jnp.float32)
    sigmoid_gate = jax.nn.sigmoid(gate_pre)
    activated = gate_pre * sigmoid_gate
    hidden_grad = jnp.einsum("slja,laf->jslf", grads_in, w_down, preferred_element_type=jnp.float32)
    up_grad = (hidden_grad * activated).astype(jnp.bfloat16)
    gate_grad = (
        hidden_grad * up_pre * sigmoid_gate * (1.0 + gate_pre * (1.0 - sigmoid_gate))
    ).astype(jnp.bfloat16)
    grad_gate = jnp.einsum("slja,jslf->laf", rows_in, gate_grad, preferred_element_type=jnp.float32)
    grad_up = jnp.einsum("slja,jslf->laf", rows_in, up_grad, preferred_element_type=jnp.float32)
    stacked_gate = gate_grad.reshape(capacity * expert_count, exp_dev, local_units)
    stacked_up = up_grad.reshape(capacity * expert_count, exp_dev, local_units)
    partial_grad = jnp.einsum(
        "rlf,laf->rla", stacked_gate, w_gate, preferred_element_type=jnp.float32
    )
    partial_grad = partial_grad + jnp.einsum(
        "rlf,laf->rla", stacked_up, w_up, preferred_element_type=jnp.float32
    )
    route_grad = lax.psum(partial_grad.astype(jnp.bfloat16), "dp")
    route_grad = route_grad.reshape(capacity, expert_count, exp_dev, features)
    returned = lax.all_to_all(route_grad, "expert", split_axis=1, concat_axis=1, tiled=True)
    returned = returned.transpose(1, 2, 0, 3).reshape(EXPERTS * capacity, features)
    picked = jnp.take(returned, target, axis=0).astype(jnp.float32)
    input_grad = jnp.sum(picked.reshape(tok_dev, per_token, features), axis=1).astype(jnp.bfloat16)
    return (input_grad, grad_gate, grad_up)


def solution(mesh):
    placed = (
        P("expert", None),
        P("expert", None),
        P("expert", None),
        P("expert", None),
        P("expert", None, "dp"),
        P("expert", None, "dp"),
        P("expert", None, "dp"),
    )
    return jax.shard_map(
        local,
        mesh=mesh,
        in_specs=placed,
        out_specs=(P("expert", None), P("expert", None, "dp"), P("expert", None, "dp")),
        check_vma=False,
    )
```

profile of v0, /device:TPU:32, one launch (start us, length us, event | category | flops | bytes accessed | tf_op | source)
XLA Modules:
  0.0 388.2 jit_solution(5050591753776055703)
XLA Ops:
  10.6 3.8 broadcast_in_dim.26
  14.4 5.9 %reshape.172 = bf16[512,3072]{1,0:T(8,128)(2,1)} reshape(bf16[128,4,3072]{2,1,0:T(4,128)(2,1)} %broadcast_in_dim.26) | data formatting | bytes 6291456 | tf_op jit(solution)/shard_map/reshape | solution.py:24
  20.3 8.6 %scatter_custom_fusion.1 = bf16[640,3072]{1,0:T(8,128)(2,1)} fusion(s32[512]{0:T(512)S(1)} %bitcast.130, bf16[512,3072]{1,0:T(8,128)(2,1)} %reshape.172, bf16[]{:T(256)} %constant.28.clone.1), kind=kCustom, calls=%fused_computation.19 | custom fusion | bytes 3932672 | tf_op jit(solution)/shard_map/scatter | solution.py:28
  28.9 4.9 %all-to-all-start.1 = ((bf16[8,1,80,3072]{3,2,1,0:T(8,128)(2,1)}), bf16[8,1,80,3072]{3,2,1,0:T(8,128)(2,1)}, u32[]{:S(2)}, u32[]{:S(2)}) async-start(bf16[8,1,80,3072]{3,2,1,0:T(8,128)(2,1)} %bitcast.127), calls=%async_computation.1 | async-start | bytes 7864320 | tf_op jit(solution)/shard_map/all_to_all | solution.py:33
  33.8 4.3 %mul.64 = f32[128,4,3072]{2,1,0:T(4,128)} broadcast(bf16[128,3072]{1,0:T(8,128)(2,1)S(1)} %copy-done.3), dimensions={0,2} | broadcast | bytes 7077888 | tf_op jit(solution)/shard_map/mul | solution.py:22
  38.1 7.8 %mul.65 = f32[512,3072]{1,0:T(8,128)} reshape(f32[128,4,3072]{2,1,0:T(4,128)} %mul.64) | data formatting | bytes 12582912 | tf_op jit(solution)/shard_map/mul | solution.py:22
  46.1 9.6 %scatter_custom_fusion = bf16[640,3072]{1,0:T(8,128)(2,1)} fusion(s32[512]{0:T(512)S(1)} %bitcast.131, f32[512,3072]{1,0:T(8,128)} %mul.65, f32[512]{0:T(512)S(1)} %mul.62, bf16[]{:T(256)} %constant.28.clone.1), kind=kCustom, calls=%fused_computation.16 | custom fusion | flops 3145728 | bytes 10225666 | tf_op jit(solution)/shard_map/scatter | solution.py:30
  55.7 24.8 %all-to-all-done.1 = bf16[8,1,80,3072]{3,2,1,0:T(8,128)(2,1)} async-done(((bf16[8,1,80,3072]{3,2,1,0:T(8,128)(2,1)}), bf16[8,1,80,3072]{3,2,1,0:T(8,128)(2,1)}, u32[]{:S(2)}, u32[]{:S(2)}) %all-to-all-start.1) | async-done | bytes 3932192 | tf_op jit(solution)/shard_map/all_to_all | solution.py:33
  80.5 4.5 %all-to-all-start = ((bf16[8,1,80,3072]{3,2,1,0:T(8,128)(2,1)}), bf16[8,1,80,3072]{3,2,1,0:T(8,128)(2,1)}, u32[]{:S(2)}, u32[]{:S(2)}) async-start(bf16[8,1,80,3072]{3,2,1,0:T(8,128)(2,1)} %bitcast.128), calls=%async_computation | async-start | bytes 7864320 | tf_op jit(solution)/shard_map/all_to_all | solution.py:34
  85.3 4.1 %fusion.30 = f32[80,8,1,256]{3,0,1,2:T(8,128)} fusion(bf16[1,3072,256]{2,1,0:T(8,128)(2,1)S(1)} %copy-done, bf16[8,1,80,3072]{3,2,1,0:T(8,128)(2,1)} %all-to-all-done.1), kind=kOutput, calls=%fused_computation.30 | convolution fusion | flops 1006632960 | bytes 6160384 | tf_op jit(solution)/shard_map/slja,laf->jslf/dot_general | solution.py:36
  89.4 42.5 %all-to-all-done = bf16[8,1,80,3072]{3,2,1,0:T(8,128)(2,1)} async-done(((bf16[8,1,80,3072]{3,2,1,0:T(8,128)(2,1)}), bf16[8,1,80,3072]{3,2,1,0:T(8,128)(2,1)}, u32[]{:S(2)}, u32[]{:S(2)}) %all-to-all-start) | async-done | bytes 3932192 | tf_op jit(solution)/shard_map/all_to_all | solution.py:34
  131.9 4.0 %multiply_convert_fusion.2 = (bf16[80,8,1,256]{3,0,1,2:T(8,128)(2,1)S(1)}, f32[80,8,1,256]{3,0,1,2:T(8,128)S(1)}) fusion(f32[80,8,1,256]{3,0,1,2:T(8,128)} %fusion.30, bf16[1,3072,256]{2,1,0:T(8,128)(2,1)} %param.13, bf16[8,1,80,3072]{3,2,1,0:T(8,128)(2,1)} %all-to-all-done), kind=kOutput, calls=%fused_computation.35 | convolution fusion | flops 1007616000 | bytes 7143424 | tf_op jit(solution)/shard_map/slja,laf->jslf/dot_general | solution.py:40
  135.9 3.5 fusion.50
  139.4 1.2 fusion.15
  140.6 1.3 fusion
  141.9 4.0 %copy.34 = bf16[80,8,1,3072]{3,0,2,1:T(8,128)(2,1)} copy(bf16[80,8,1,3072]{3,1,0,2:T(8,128)(2,1)S(1)} %fusion) | data formatting | bytes 7864320 | tf_op jit(solution)/shard_map/reshape | solution.py:56
  146.0 161.8 %all-reduce.2.cloned.1.call-done = bf16[80,8,1,3072]{3,0,2,1:T(8,128)(2,1)} async-done(((bf16[80,8,1,3072]{3,0,2,1:T(8,128)(2,1)}), bf16[80,8,1,3072]{3,0,2,1:T(8,128)(2,1)}) %all-reduce.2.cloned.1.call-update) | async-done | bytes 3932176 | tf_op jit(solution)/shard_map/psum | solution.py:55
  307.8 4.8 %all-to-all-start.2 = ((bf16[80,8,1,3072]{3,0,2,1:T(8,128)(2,1)}), bf16[80,8,1,3072]{3,0,2,1:T(8,128)(2,1)}, u32[]{:S(2)}, u32[]{:S(2)}) async-start(bf16[80,8,1,3072]{3,0,2,1:T(8,128)(2,1)} %all-reduce.2.cloned.1.call-done), calls=%async_computation.2 | async-start | bytes 7864320 | tf_op jit(solution)/shard_map/all_to_all | solution.py:57
  313.0 5.2 %convolution_bitcast_fusion.1 = f32[1,3072,256]{2,1,0:T(8,128)} fusion(bf16[8,1,80,3072]{3,2,1,0:T(8,128)(2,1)} %all-to-all-done.1, bf16[80,8,1,256]{3,0,1,2:T(8,128)(2,1)S(1)} %fusion.50), kind=kOutput, calls=%fused_computation.7 | convolution fusion | flops 1006632960 | bytes 7405568 | tf_op jit(solution)/shard_map/slja,jslf->laf/dot_general | solution.py:45
  318.2 5.2 %convolution_bitcast_fusion = f32[1,3072,256]{2,1,0:T(8,128)} fusion(bf16[8,1,80,3072]{3,2,1,0:T(8,128)(2,1)} %all-to-all-done.1, bf16[80,8,1,256]{3,0,1,2:T(8,128)(2,1)S(1)} %copy-done.5), kind=kOutput, calls=%fused_computation.6 | convolution fusion | flops 1006632960 | bytes 7405568 | tf_op jit(solution)/shard_map/slja,jslf->laf/dot_general | solution.py:46
  323.4 35.8 %all-to-all-done.2 = bf16[80,8,1,3072]{3,0,2,1:T(8,128)(2,1)} async-done(((bf16[80,8,1,3072]{3,0,2,1:T(8,128)(2,1)}), bf16[80,8,1,3072]{3,0,2,1:T(8,128)(2,1)}, u32[]{:S(2)}, u32[]{:S(2)}) %all-to-all-start.2) | async-done | bytes 3932192 | tf_op jit(solution)/shard_map/all_to_all | solution.py:57
  359.2 9.8 %gather_fusion = bf16[512,3072]{1,0:T(8,128)(2,1)} fusion(bf16[640,3072]{1,0:T(8,128)(2,1)} %bitcast.34, s32[1024]{0:T(1024)S(1)} %pad_clamp_fusion), kind=kCustom, calls=%fused_computation | custom fusion | bytes 6293504 | tf_op jit(solution)/shard_map/jit(_take)/gather | solution.py:59
  369.0 6.1 %gather.7 = bf16[128,4,3072]{2,1,0:T(4,128)(2,1)} reshape(bf16[512,3072]{1,0:T(8,128)(2,1)} %gather_fusion) | data formatting | bytes 6291456 | tf_op jit(solution)/shard_map/jit(_take)/gather | solution.py:59
  375.1 6.2 %select_reduce_fusion = bf16[128,3072]{1,0:T(8,128)(2,1)} fusion(bf16[128,4,3072]{2,1,0:T(4,128)(2,1)} %gather.7, pred[128,4]{1,0:T(8,128)(4,1)S(1)} %copy.29), kind=kLoop, calls=%fused_computation.17 | loop fusion | flops 2752512 | bytes 3932672 | tf_op jit(solution)/shard_map/reduce_sum | solution.py:60
  (40 shorter events, 4.4 us)
Async XLA Ops:
  7.2 78.1 %copy-start = (bf16[1,3072,256]{2,1,0:T(8,128)(2,1)S(1)}, bf16[1,3072,256]{2,1,0:T(8,128)(2,1)}, u32[]{:S(2)}) copy-start(bf16[1,3072,256]{2,1,0:T(8,128)(2,1)} %param.11) | copy-start | bytes 4718596
  28.9 4.9 %copy-start.3 = (bf16[128,3072]{1,0:T(8,128)(2,1)S(1)}, bf16[128,3072]{1,0:T(8,128)(2,1)}, u32[]{:S(2)}) copy-start(bf16[128,3072]{1,0:T(8,128)(2,1)} %param.7) | copy-start | bytes 2359300
  28.9 51.6 %all-to-all-start.1 = ((bf16[8,1,80,3072]{3,2,1,0:T(8,128)(2,1)}), bf16[8,1,80,3072]{3,2,1,0:T(8,128)(2,1)}, u32[]{:S(2)}, u32[]{:S(2)}) async-start(bf16[8,1,80,3072]{3,2,1,0:T(8,128)(2,1)} %bitcast.127), calls=%async_computation.1 | async-start | bytes 7864320 | tf_op jit(solution)/shard_map/all_to_all | solution.py:33
  38.1 7.8 %copy-start.7 = (f32[128,4]{0,1:T(4,128)S(1)}, f32[128,4]{0,1:T(4,128)}, u32[]{:S(2)}) copy-start(f32[128,4]{0,1:T(4,128)} %param.9) | copy-start | bytes 6148
  80.5 51.4 %all-to-all-start = ((bf16[8,1,80,3072]{3,2,1,0:T(8,128)(2,1)}), bf16[8,1,80,3072]{3,2,1,0:T(8,128)(2,1)}, u32[]{:S(2)}, u32[]{:S(2)}) async-start(bf16[8,1,80,3072]{3,2,1,0:T(8,128)(2,1)} %bitcast.128), calls=%async_computation | async-start | bytes 7864320 | tf_op jit(solution)/shard_map/all_to_all | solution.py:34
  85.0 222.8 %all-reduce.2.cloned.1.call-start = ((), (), s32[]{:S(2)}) async-start(), calls=%async_computation.3 | async-start | bytes 7864320 | tf_op jit(solution)/shard_map/psum | solution.py:55
  89.4 46.4 %copy-start.2 = (bf16[1,3072,256]{2,1,0:T(8,128)(2,1)S(1)}, bf16[1,3072,256]{2,1,0:T(8,128)(2,1)}, u32[]{:S(2)}) copy-start(bf16[1,3072,256]{2,1,0:T(8,128)(2,1)} %param.12) | copy-start | bytes 4718596
  131.9 4.0 %copy-start.8 = (f32[80,8,1,256]{3,0,1,2:T(8,128)S(1)}, f32[80,8,1,256]{3,0,1,2:T(8,128)}, u32[]{:S(2)}) copy-start(f32[80,8,1,256]{3,0,1,2:T(8,128)} %fusion.30) | copy-start | bytes 1966084
  135.8 4.8 %copy-start.4 = (bf16[80,8,1,256]{3,0,1,2:T(8,128)(2,1)}, bf16[80,8,1,256]{3,0,1,2:T(8,128)(2,1)S(1)}, u32[]{:S(2)}) copy-start(bf16[80,8,1,256]{3,0,1,2:T(8,128)(2,1)S(1)} %get-tuple-element.3) | copy-start | bytes 983044
  146.0 166.8 %copy-start.6 = (s32[128,4]{0,1:T(4,128)S(1)}, s32[128,4]{0,1:T(4,128)}, u32[]{:S(2)}) copy-start(s32[128,4]{0,1:T(4,128)} %param.8) | copy-start | bytes 6148
  307.8 51.4 %all-to-all-start.2 = ((bf16[80,8,1,3072]{3,0,2,1:T(8,128)(2,1)}), bf16[80,8,1,3072]{3,0,2,1:T(8,128)(2,1)}, u32[]{:S(2)}, u32[]{:S(2)}) async-start(bf16[80,8,1,3072]{3,0,2,1:T(8,128)(2,1)} %all-reduce.2.cloned.1.call-done), calls=%async_computation.2 | async-start | bytes 7864320 | tf_op jit(solution)/shard_map/all_to_all | solution.py:57
  313.0 5.3 %copy-start.5 = (bf16[80,8,1,256]{3,0,1,2:T(8,128)(2,1)S(1)}, bf16[80,8,1,256]{3,0,1,2:T(8,128)(2,1)}, u32[]{:S(2)}) copy-start(bf16[80,8,1,256]{3,0,1,2:T(8,128)(2,1)} %copy-done.4) | copy-start | bytes 983044
  359.2 22.1 %copy-start.1 = (bf16[1,3072,256]{2,1,0:T(8,128)(2,1)S(1)}, bf16[1,3072,256]{2,1,0:T(8,128)(2,1)}, u32[]{:S(2)}) copy-start(bf16[1,3072,256]{2,1,0:T(8,128)(2,1)} %param.11) | copy-start | bytes 4718596
Sparse Core Ops, SparseCore 0:
  146.1 161.6 all-reduce.1
where the time goes:
time: 391 us; the launch traced here: 388 us
  waiting for transfers between devices  265 us (68%)
  local copies, waits for them, and re-layouts  52.4 us (13%)
  matrix products  24.5 us (6%)
  other arithmetic  17.8 us (5%)
  starting transfers between devices  14.4 us (4%)
  between operations  14.2 us (4%)
    psum x1, waiting for transfers between devices, local(): route_grad = lax.psum(partial_grad.astype(jnp.bfloat16), 'dp')  162 us
    all_to_all x1, waiting for transfers between devices, local(): lax.all_to_all(grads_out, 'expert', split_axis=0, concat_axis=0, tiled=True)  42.5 us
    all_to_all x1, waiting for transfers between devices, local(): lax.all_to_all(route_grad, 'expert', split_axis=1, concat_axis=1, tiled=T...  35.8 us
    all_to_all x1, waiting for transfers between devices, local(): lax.all_to_all(rows_out, 'expert', split_axis=0, concat_axis=0, tiled=True)  24.8 us
    gather x2, local copies, waits for them, and re-layouts, local(): picked = jnp.take(returned, target, axis=0).astype(jnp.float32)  15.9 us
    mul x3, local copies, waits for them, and re-layouts, local(): scaled = gate_values[:, :, None] * out_grad[:, None, :].astype(jnp.float32)  12.2 us
    scatter x1, other arithmetic, local(): blank_slots.at[target].set(scaled)  9.6 us
    scatter x1, local copies, waits for them, and re-layouts, local(): blank_slots.at[target].set(copies)  8.57 us
  transfers between devices with their start and end apart: 4, of which 4 were waited for; matrix products, arithmetic and copies ran while one was open for 9% of the time, Pallas kernels for 0%

commit v1 on v0

v1 whole, which is shorter than its diff:
```python
import jax
import jax.numpy as jnp
from jax import lax
from jax.sharding import PartitionSpec as P

EXPERTS = 8


def local(out_grad, routes, gate_values, layer_input, w_gate, w_up, w_down):
    me = lax.axis_index("expert")
    w_gate, w_up, w_down = w_gate[0], w_up[0], w_down[0]
    experts_row = jnp.arange(EXPERTS, dtype=jnp.int32)
    dense = jnp.sum(
        jnp.where(routes[:, :, None] == experts_row, gate_values[:, :, None], 0.0), axis=1
    )
    weight = lax.all_gather(dense, "expert", axis=0, tiled=True)
    weight = lax.dynamic_slice_in_dim(weight, me, 1, axis=1)
    rows = lax.all_gather(layer_input, "expert", axis=0, tiled=True)
    grads = lax.all_gather(out_grad, "expert", axis=0, tiled=True)
    gate_pre = jnp.dot(rows, w_gate, preferred_element_type=jnp.float32)
    up_pre = jnp.dot(rows, w_up, preferred_element_type=jnp.float32)
    hidden_grad = weight * jnp.dot(grads, w_down, preferred_element_type=jnp.float32)
    sigmoid_gate = jax.nn.sigmoid(gate_pre)
    activated = gate_pre * sigmoid_gate
    up_grad = (hidden_grad * activated).astype(jnp.bfloat16)
    gate_grad = (
        hidden_grad * up_pre * sigmoid_gate * (1.0 + gate_pre * (1.0 - sigmoid_gate))
    ).astype(jnp.bfloat16)
    partial = jnp.dot(gate_grad, w_gate.T, preferred_element_type=jnp.float32)
    partial = partial + jnp.dot(up_grad, w_up.T, preferred_element_type=jnp.float32)
    total = lax.psum_scatter(partial.astype(jnp.bfloat16), "expert", scatter_dimension=0, tiled=True)
    total = lax.psum(total, "dp")
    grad_gate = jnp.dot(rows.T, gate_grad, preferred_element_type=jnp.float32)
    grad_up = jnp.dot(rows.T, up_grad, preferred_element_type=jnp.float32)
    return total, grad_gate[None], grad_up[None]


def solution(mesh):
    placed = (
        P("expert", None),
        P("expert", None),
        P("expert", None),
        P("expert", None),
        P("expert", None, "dp"),
        P("expert", None, "dp"),
        P("expert", None, "dp"),
    )
    return jax.shard_map(
        local,
        mesh=mesh,
        in_specs=placed,
        out_specs=(P("expert", None), P("expert", None, "dp"), P("expert", None, "dp")),
        check_vma=False,
    )
```

time: 391 us -> 322 us (0.82)
  local copies, waits for them, and re-layouts: 52.4 us -> 9.7 us
  other arithmetic: 17.8 us -> 0.71 us
  waiting for transfers between devices: 265 us -> 250 us
  starting transfers between devices: 14.4 us -> 0.34 us
  blocking collectives: 0 us -> 13.3 us
  matrix products: 24.5 us -> 32 us
    all_to_all x3 -> x0, waiting for transfers between devices: 103 us -> none  [the longest x1 42.5 us: local(): lax.all_to_all(grads_out, 'expert', split_axis=0, concat_axis=0, tiled=True)]
    all_gather x0 -> x2, waiting for transfers between devices: none -> 73.1 us  [the longest x1 39.9 us: local(): grads = lax.all_gather(out_grad, 'expert', axis=0, tiled=True)]
    reduce_scatter x0 -> x1, waiting for transfers between devices: none -> 45.1 us  [local(): lax.psum_scatter(partial.astype(jnp.bfloat16), 'expert', scatter_dimensio...]
    psum x1, waiting for transfers between devices: 162 us -> 131 us  [local(): total = lax.psum(total, 'dp')]
    gather x2 -> x0, local copies, waits for them, and re-layouts: 15.9 us -> none  [local(): picked = jnp.take(returned, target, axis=0).astype(jnp.float32)]
    all_to_all x3 -> x0, starting transfers between devices: 14.1 us -> none  [the longest x1 4.87 us: local(): lax.all_to_all(rows_out, 'expert', split_axis=0, concat_axis=0, tiled=True)]
    all_gather x0 -> x1, blocking collectives: none -> 13.3 us  [local(): weight = lax.all_gather(dense, 'expert', axis=0, tiled=True)]
    mul x5 -> x0, local copies, waits for them, and re-layouts: 12.4 us -> none  [the longest x3 12.2 us: local(): scaled = gate_values[:, :, None] * out_grad[:, None, :].astype(jnp.float32)]
  transfers between devices with their start and end apart: 4 -> 4, of which waited for: 4 -> 4; matrix products, arithmetic and copies ran while one was open for 9% -> 8% of each run, Pallas kernels for 0% -> 0%
where the time goes in v1:
time: 322 us; the launch traced here: 320 us
  waiting for transfers between devices  250 us (78%)
  matrix products  32 us (10%)
  between operations  13.8 us (4%)
  blocking collectives  13.3 us (4%)
  local copies, waits for them, and re-layouts  9.7 us (3%)
    psum x1, waiting for transfers between devices, local(): total = lax.psum(total, 'dp')  131 us
    reduce_scatter x1, waiting for transfers between devices, local(): lax.psum_scatter(partial.astype(jnp.bfloat16), 'expert', scatter_dimensio...  45.1 us
    all_gather x1, waiting for transfers between devices, local(): grads = lax.all_gather(out_grad, 'expert', axis=0, tiled=True)  39.9 us
    all_gather x1, waiting for transfers between devices, local(): rows = lax.all_gather(layer_input, 'expert', axis=0, tiled=True)  33.2 us
    all_gather x1, blocking collectives, local(): weight = lax.all_gather(dense, 'expert', axis=0, tiled=True)  13.3 us
    unnamed x11, local copies, waits for them, and re-layouts  9.69 us
  transfers between devices with their start and end apart: 4, of which 4 were waited for; matrix products, arithmetic and copies ran while one was open for 8% of the time, Pallas kernels for 0%

profile of v1, /device:TPU:32, one launch (start us, length us, event | category | flops | bytes accessed | tf_op | source)
XLA Modules:
  0.0 320.2 jit_solution(17228274745104250049)
XLA Ops:
  7.2 0.0 all-gather.5.cloned.1.call-start
  7.2 0.7 all-gather.5.cloned.1.call-update
  7.9 0.0 all-gather.3.cloned.1.call-start
  8.0 0.7 all-gather.3.cloned.1.call-update
  8.7 0.0 reduce-scatter.2.cloned.1.call-start
  8.7 0.7 select_reduce_fusion
  9.4 13.3 %all_gather.9 = f32[1024,8]{0,1:T(8,128)S(1)} all-gather(f32[128,8]{0,1:T(8,128)S(1)} %select_reduce_fusion), channel_id=1, replica_groups=mesh['dp'=32,'expert'=8] {'expert'}, dimensions={0}, use_global_device_ids=true | all-gather | bytes 36864 | tf_op jit(solution)/shard_map/all_gather | solution.py:16
  22.8 33.2 %all-gather.5.cloned.1.call-done = bf16[1024,3072]{1,0:T(8,128)(2,1)} async-done(((bf16[128,3072]{1,0:T(8,128)(2,1)}), bf16[1024,3072]{1,0:T(8,128)(2,1)}) %all-gather.5.cloned.1.call-update) | async-done | bytes 6291472 | tf_op jit(solution)/shard_map/all_gather | solution.py:18
  56.0 5.5 %fusion.2 = f32[1024,256]{1,0:T(8,128)} fusion(bf16[1024,3072]{1,0:T(8,128)(2,1)} %all-gather.5.cloned.1.call-done, bf16[1,3072,256]{2,1,0:T(8,128)(2,1)S(1)} %copy-done), kind=kOutput, calls=%fused_computation.5 | convolution fusion | flops 1610612736 | bytes 8912896 | tf_op jit(solution)/shard_map/dot_general | solution.py:20
  61.5 39.9 %all-gather.3.cloned.1.call-done = bf16[1024,3072]{1,0:T(8,128)(2,1)} async-done(((bf16[128,3072]{1,0:T(8,128)(2,1)}), bf16[1024,3072]{1,0:T(8,128)(2,1)}) %all-gather.3.cloned.1.call-update) | async-done | bytes 6291472 | tf_op jit(solution)/shard_map/all_gather | solution.py:19
  101.4 5.5 %multiply_convert_fusion = (bf16[1024,256]{1,0:T(8,128)(2,1)S(1)}, f32[1024,256]{1,0:T(8,128)S(1)}) fusion(f32[1024,256]{1,0:T(8,128)} %fusion.2, bf16[1024,3072]{1,0:T(8,128)(2,1)} %all-gather.3.cloned.1.call-done, bf16[1,3072,256]{2,1,0:T(8,128)(2,1)} %param.13, f32[1024]{0:T(1024)S(1)} %bitcast.43), kind=kOutput, calls=%fused_computation.17 | convolution fusion | flops 1612447744 | bytes 10489856 | tf_op jit(solution)/shard_map/dot_general | solution.py:22
  106.9 0.3 copy-done.2
  107.2 0.3 copy-done.3
  107.5 2.0 fusion.21
  109.4 1.8 fusion
  111.3 4.6 %add_convert_fusion = bf16[1024,3072]{1,0:T(8,128)(2,1)} fusion(f32[1024,3072]{1,0:T(8,128)S(1)} %fusion, bf16[1024,256]{1,0:T(8,128)(2,1)S(1)} %get-tuple-element.12, bf16[1,3072,256]{2,1,0:T(8,128)(2,1)S(1)} %copy-done.2), kind=kOutput, calls=%fused_computation | convolution fusion | flops 1616904192 | bytes 20971520 | tf_op jit(solution)/shard_map/dot_general | solution.py:30
  115.9 0.2 all-reduce.2.cloned.1.call-start
  116.1 45.1 %reduce-scatter.2.cloned.1.call-done = bf16[128,3072]{1,0:T(8,128)(2,1)} async-done(((bf16[1024,3072]{1,0:T(8,128)(2,1)}), bf16[128,3072]{1,0:T(8,128)(2,1)}) %reduce-scatter.2.cloned.1.call-update) | async-done | bytes 786448 | tf_op jit(solution)/shard_map/reduce_scatter | solution.py:31
  161.2 6.3 %convolution_bitcast_fusion = f32[1,3072,256]{1,2,0:T(8,128)} fusion(bf16[1024,256]{1,0:T(8,128)(2,1)S(1)} %get-tuple-element.12, bf16[1024,3072]{1,0:T(8,128)(2,1)} %all-gather.5.cloned.1.call-done), kind=kOutput, calls=%fused_computation.1 | convolution fusion | flops 1610612736 | bytes 9961472 | tf_op jit(solution)/shard_map/dot_general | solution.py:34
  167.5 3.5 %copy.19 = f32[1,3072,256]{2,1,0:T(8,128)} copy(f32[1,3072,256]{1,2,0:T(8,128)} %convolution_bitcast_fusion) | data formatting | bytes 6291456
  171.0 6.3 %convolution_bitcast_fusion.1 = f32[1,3072,256]{1,2,0:T(8,128)} fusion(bf16[1024,256]{1,0:T(8,128)(2,1)S(1)} %fusion.21, bf16[1024,3072]{1,0:T(8,128)(2,1)} %all-gather.5.cloned.1.call-done), kind=kOutput, calls=%fused_computation.2 | convolution fusion | flops 1610612736 | bytes 9961472 | tf_op jit(solution)/shard_map/dot_general | solution.py:33
  177.3 3.5 %copy.18 = f32[1,3072,256]{2,1,0:T(8,128)} copy(f32[1,3072,256]{1,2,0:T(8,128)} %convolution_bitcast_fusion.1) | data formatting | bytes 6291456
  180.9 130.7 %all-reduce.2.cloned.1.call-done = bf16[128,3072]{1,0:T(8,128)(2,1)} async-done(((bf16[128,3072]{1,0:T(8,128)(2,1)}), bf16[128,3072]{1,0:T(8,128)(2,1)}) %all-reduce.2.cloned.1.call-update) | async-done | bytes 786448 | tf_op jit(solution)/shard_map/psum | solution.py:32
  311.6 2.1 copy.21
  (9 shorter events, 0.1 us)
Async XLA Ops:
  7.2 48.8 %copy-start = (bf16[1,3072,256]{2,1,0:T(8,128)(2,1)S(1)}, bf16[1,3072,256]{2,1,0:T(8,128)(2,1)}, u32[]{:S(2)}) copy-start(bf16[1,3072,256]{2,1,0:T(8,128)(2,1)} %param.11) | copy-start | bytes 4718596
  7.2 48.8 %all-gather.5.cloned.1.call-start = ((), (), s32[]{:S(2)}) async-start(), calls=%async_computation.2 | async-start | bytes 7077888 | tf_op jit(solution)/shard_map/all_gather | solution.py:18
  7.9 93.5 %all-gather.3.cloned.1.call-start = ((), (), s32[]{:S(2)}) async-start(), calls=%async_computation.1 | async-start | bytes 7077888 | tf_op jit(solution)/shard_map/all_gather | solution.py:19
  8.7 152.5 %reduce-scatter.2.cloned.1.call-start = ((), (), s32[]{:S(2)}) async-start(), calls=%async_computation.3 | async-start | bytes 7077888 | tf_op jit(solution)/shard_map/reduce_scatter | solution.py:31
  101.4 5.5 %copy-start.1 = (bf16[1024,3072]{1,0:T(8,128)(2,1)S(1)}, bf16[1024,3072]{1,0:T(8,128)(2,1)}, u32[]{:S(2)}) copy-start(bf16[1024,3072]{1,0:T(8,128)(2,1)} %all-gather.5.cloned.1.call-done) | copy-start | bytes 18874372
  101.4 5.8 %copy-start.2 = (bf16[1,3072,256]{2,1,0:T(8,128)(2,1)S(1)}, bf16[1,3072,256]{2,1,0:T(8,128)(2,1)}, u32[]{:S(2)}) copy-start(bf16[1,3072,256]{2,1,0:T(8,128)(2,1)} %param.12) | copy-start | bytes 4718596
  101.4 6.0 %copy-start.3 = (f32[1024,256]{1,0:T(8,128)S(1)}, f32[1024,256]{1,0:T(8,128)}, u32[]{:S(2)}) copy-start(f32[1024,256]{1,0:T(8,128)} %fusion.2) | copy-start | bytes 3145732
  115.9 195.7 %all-reduce.2.cloned.1.call-start = ((), (), s32[]{:S(2)}) async-start(), calls=%async_computation.4 | async-start | bytes 1572864 | tf_op jit(solution)/shard_map/psum | solution.py:32
Sparse Core Ops, SparseCore 0:
  9.8 46.0 all-gather.4
  57.8 43.5 all-gather.2
  116.0 45.1 reduce-scatter.1
  164.4 147.1 all-reduce.1

commit v2 on v1

v2 whole, which is shorter than its diff:
```python
import functools

import jax
import jax.numpy as jnp
from jax import lax
from jax.experimental import pallas as pl
from jax.experimental.pallas import tpu as pltpu
from jax.sharding import PartitionSpec as P

MESH = pl.DeviceIdType.MESH
BF16, F32 = jnp.bfloat16, jnp.float32
EXPERTS = 8
NX, NY, NZ = 4, 4, 8
TOK, D, U = 128, 3072, 256
HALF = TOK // 2
XROWS = HALF // NX
ZCOLS = D // NZ
OWN, UP, DOWN, FAR = 0, 1, 2, 3
TILE = 256


def kernel(
    og_in, routes_in, gates_in, x_in, wg_in, wu_in, wd_in,
    out_hbm, gg_hbm, gu_hbm,
    xo, wgu, wd, g8, dg, ps, pr, s, xr, u, zr, v, yr, out, grads,
    load_sem, send_sem, recv_sem, grad_sem,
):
    dp, ex = lax.axis_index("dp"), lax.axis_index("expert")
    x, z = lax.rem(dp, NX), lax.div(dp, NX)
    y, c = lax.div(ex, 2), lax.rem(ex, 2)

    def dev(nx, ny, nz, nc):
        return (nz * NX + nx, ny * 2 + nc)

    sib = dev(x, y, z, 1 - c)
    y_at = {d: lax.rem(y + d, NY) for d in (1, 2, 3)}
    x_at = {d: lax.rem(x + d, NX) for d in (1, 2, 3)}
    z_at = {d: lax.rem(z + d, NZ) for d in range(1, NZ)}
    to_y = {d: dev(x, y_at[d], z, c) for d in y_at}
    to_x = {d: dev(x_at[d], y, z, c) for d in x_at}
    to_z = {d: dev(x, y, z_at[d], c) for d in z_at}

    loads = []

    def load(src, dst):
        copy = pltpu.make_async_copy(src, dst, load_sem.at[len(loads)])
        copy.start()
        loads.append(copy)
        return copy

    sent = []

    def send(src, dst, device):
        i = len(sent)
        copy = pltpu.make_async_remote_copy(
            src_ref=src, dst_ref=dst, send_sem=send_sem.at[i], recv_sem=recv_sem.at[i],
            device_id=device, device_id_type=MESH,
        )
        copy.start()
        sent.append(copy)
        return copy

    own_loads = {}
    for h in range(2):
        for a, ref in ((0, x_in), (1, og_in)):
            own_loads[a, h] = load(ref.at[pl.ds(h * HALF, HALF)], xo.at[a, h, OWN, 0])
    weight_loads = [
        load(wg_in.at[0], wgu.at[:, pl.ds(0, U)]),
        load(wu_in.at[0], wgu.at[:, pl.ds(U, U)]),
        load(wd_in.at[0], wd),
    ]

    peers = [sib] + list(to_y.values()) + list(to_x.values()) + list(to_z.values())
    barrier = pltpu.get_barrier_semaphore()
    for device in peers:
        pl.semaphore_signal(barrier, inc=1, device_id=device, device_id_type=MESH)

    lane = lax.broadcasted_iota(jnp.int32, (TOK, TOK), 1)
    row = lax.broadcasted_iota(jnp.int32, (TOK, TOK), 0)
    for e in range(EXPERTS):
        column = jnp.sum(jnp.where(routes_in[...] == e, gates_in[...], 0.0), axis=1, keepdims=True)
        g8[OWN, 0, e : e + 1, :] = jnp.sum(jnp.where(lane == row, column, 0.0), axis=0, keepdims=True)

    pl.semaphore_wait(barrier, len(peers))

    g_move = {
        DOWN: send(g8.at[OWN, 0], g8.at[DOWN, 0], to_y[1]),
        UP: send(g8.at[OWN, 0], g8.at[UP, 0], to_y[3]),
        FAR: send(g8.at[OWN, 0], g8.at[FAR, 0], to_y[2]),
    }
    g_swap = {OWN: send(g8.at[OWN, 0], g8.at[OWN, 1], sib)}
    move, swap = {}, {}

    def send_own(h):
        for a in (0, 1):
            move[a, h, DOWN] = send(xo.at[a, h, OWN, 0], xo.at[a, h, DOWN, 0], to_y[1])
            b = 1 - a
            move[b, h, UP] = send(xo.at[b, h, OWN, 0], xo.at[b, h, UP, 0], to_y[3])

    def do_swap(a, h, j):
        swap[a, h, j] = send(xo.at[a, h, j, 0], xo.at[a, h, j, 1], sib)

    for a in range(2):
        own_loads[a, 0].wait()
    send_own(0)
    for h in range(2):
        for a in range(2):
            if h:
                own_loads[a, h].wait()
            do_swap(a, h, OWN)

    def first_pieces(h):
        move[0, h, DOWN].wait_recv()
        move[0, h, FAR] = send(xo.at[0, h, DOWN, 0], xo.at[0, h, FAR, 0], to_y[1])
        move[1, h, UP].wait_recv()
        move[1, h, FAR] = send(xo.at[1, h, UP, 0], xo.at[1, h, FAR, 0], to_y[3])
        do_swap(0, h, DOWN)
        do_swap(1, h, UP)

    def second_pieces(h):
        move[1, h, DOWN].wait_recv()
        do_swap(1, h, DOWN)
        move[0, h, UP].wait_recv()
        do_swap(0, h, UP)

    def far_pieces(h):
        for a in range(2):
            move[a, h, FAR].wait_recv()
            do_swap(a, h, FAR)

    def weight_column(h, j, slot):
        mine = lax.broadcasted_iota(jnp.int32, (EXPERTS, TOK), 0) == ex
        line = jnp.sum(jnp.where(mine, g8[j, slot], 0.0), axis=0, keepdims=True)
        whole = jnp.sum(jnp.where(lane == row, line, 0.0), axis=1, keepdims=True)
        return whole[h * HALF : (h + 1) * HALF]

    def compute(h, j, n):
        rows = n * TOK
        for jj in range(j, j + n):
            for a in range(2):
                swap[a, h, jj].wait_recv()
        weight = jnp.concatenate(
            [weight_column(h, jj, slot) for jj in range(j, j + n) for slot in range(2)], axis=0
        )
        tokens = xo[0, h, j : j + n].reshape(rows, D)
        gate_pre = jnp.dot(tokens, wgu[:, :U], preferred_element_type=F32)
        up_pre = jnp.dot(tokens, wgu[:, U:], preferred_element_type=F32)
        grads_in = xo[1, h, j : j + n].reshape(rows, D)
        hidden = weight * jnp.dot(grads_in, wd[...], preferred_element_type=F32)
        sig = jax.nn.sigmoid(gate_pre)
        up_grad = (hidden * (gate_pre * sig)).astype(BF16)
        gate_grad = (hidden * up_pre * sig * (1.0 + gate_pre * (1.0 - sig))).astype(BF16)
        both = jnp.concatenate([gate_grad, up_grad], axis=1)
        dg[h, j : j + n] = both.reshape(n, 2, HALF, 2 * U)

        def tile(i, carry):
            cols = pl.ds(pl.multiple_of(i * TILE, TILE), TILE)
            part = lax.dot_general(
                dg[h, j : j + n].reshape(rows, 2 * U), wgu[cols, :], (((1,), (1,)), ((), ())),
                preferred_element_type=F32,
            ).astype(BF16).reshape(n, 2, HALF, TILE)
            s[h, j : j + n, :, cols] = part[:, 0]
            ps[h, j : j + n, :, cols] = part[:, 1]
            return carry

        lax.fori_loop(0, D // TILE, tile, 0)

    def swap_parts(h, j, n):
        return send(ps.at[h, pl.ds(j, n)], pr.at[h, pl.ds(j, n)], sib)

    def scatter_x(h, j, n, swapped):
        swapped.wait_recv()
        for jj in range(j, j + n):
            s[h, jj] = (s[h, jj].astype(F32) + pr[h, jj].astype(F32)).astype(BF16)
        got = []
        for d in (1, 3, 2):
            rows = pl.ds(pl.multiple_of(x_at[d] * XROWS, XROWS), XROWS)
            got.append(
                send(s.at[h, pl.ds(j, n), rows], xr.at[d - 1, h, pl.ds(j, n)], to_x[d])
            )
        return got

    def sum_x(h, j, n, got):
        for copy in got:
            copy.wait_recv()
        rows = pl.ds(pl.multiple_of(x * XROWS, XROWS), XROWS)
        for jj in range(j, j + n):
            total = s[h, jj, rows].astype(F32)
            for d in range(3):
                total = total + xr[d, h, jj].astype(F32)
            u[h, jj] = total.astype(BF16)

    def scatter_z(h, j, n):
        got = []
        for d in (1, 7, 2, 6, 3, 5, 4):
            cols = pl.ds(pl.multiple_of(z_at[d] * ZCOLS, ZCOLS), ZCOLS)
            got.append(
                send(u.at[h, pl.ds(j, n), :, cols], zr.at[d - 1, h, pl.ds(j, n)], to_z[d])
            )
        return got

    my_cols = pl.ds(pl.multiple_of(z * ZCOLS, ZCOLS), ZCOLS)

    def sum_z(h, j, n, got):
        for copy in got:
            copy.wait_recv()
        for jj in range(j, j + n):
            total = u[h, jj, :, my_cols].astype(F32)
            for d in range(NZ - 1):
                total = total + zr[d, h, jj].astype(F32)
            v[h, jj] = total.astype(BF16)

    def scatter_y(h):
        return [
            send(v.at[h, j], yr.at[h, j - 1], to_y[d])
            for j, d in ((UP, 1), (DOWN, 3), (FAR, 2))
        ]

    def place(h):
        return pl.ds(pl.multiple_of(h * HALF + x * XROWS, XROWS), XROWS)

    def gather_z(h, got):
        for copy in got:
            copy.wait_recv()
        total = v[h, OWN].astype(F32)
        for j in range(3):
            total = total + yr[h, j].astype(F32)
        out[place(h), my_cols] = total.astype(BF16)
        piece = out.at[place(h), my_cols]
        return [send(piece, piece, to_z[d]) for d in (1, 7, 2, 6, 3, 5, 4)]

    def gather_x(h, got):
        for copy in got:
            copy.wait_recv()
        piece = out.at[place(h)]
        return [send(piece, piece, to_x[d]) for d in (1, 3, 2)]

    grad_copies = []

    def grad_tiles(first, last):
        def tile(i, carry):
            cols = pl.ds(pl.multiple_of(i * TILE, TILE), TILE)
            part = lax.dot_general(
                xo[0, :, :, :, :, cols].reshape(8 * TOK, TILE),
                dg[...].reshape(8 * TOK, 2 * U),
                (((0,), (0,)), ((), ())),
                preferred_element_type=F32,
            )
            grads[0, cols] = part[:, :U]
            grads[1, cols] = part[:, U:]
            return carry

        lax.fori_loop(first, last, tile, 0)
        rows = pl.ds(first * TILE, (last - first) * TILE)
        for k, ref in enumerate((gg_hbm, gu_hbm)):
            copy = pltpu.make_async_copy(
                grads.at[k, rows], ref.at[0, rows], grad_sem.at[len(grad_copies)]
            )
            copy.start()
            grad_copies.append(copy)

    g_swap[OWN].wait_recv()
    for copy in weight_loads:
        copy.wait()
    compute(0, OWN, 1)
    p_own0 = swap_parts(0, OWN, 1)
    compute(1, OWN, 1)
    p_own1 = swap_parts(1, OWN, 1)
    for j in (UP, DOWN, FAR):
        g_move[j].wait_recv()
        g_swap[j] = send(g8.at[j, 0], g8.at[j, 1], sib)
    first_pieces(0)
    send_own(1)
    x_own0 = scatter_x(0, OWN, 1, p_own0)
    x_own1 = scatter_x(1, OWN, 1, p_own1)
    for j in (UP, DOWN, FAR):
        g_swap[j].wait_recv()
    second_pieces(0)
    compute(0, UP, 2)
    p_mid0 = swap_parts(0, UP, 2)
    sum_x(0, OWN, 1, x_own0)
    x_mid0 = scatter_x(0, UP, 2, p_mid0)
    sum_x(1, OWN, 1, x_own1)
    far_pieces(0)
    compute(0, FAR, 1)
    p_far0 = swap_parts(0, FAR, 1)
    sum_x(0, UP, 2, x_mid0)
    z_mid0 = scatter_z(0, OWN, 3)
    x_far0 = scatter_x(0, FAR, 1, p_far0)
    first_pieces(1)
    sum_x(0, FAR, 1, x_far0)
    z_far0 = scatter_z(0, FAR, 1)
    sum_z(0, OWN, 3, z_mid0)
    sum_z(0, FAR, 1, z_far0)
    y_0 = scatter_y(0)
    second_pieces(1)
    compute(1, UP, 2)
    p_mid1 = swap_parts(1, UP, 2)
    zg_0 = gather_z(0, y_0)
    x_mid1 = scatter_x(1, UP, 2, p_mid1)
    xg_0 = gather_x(0, zg_0)
    far_pieces(1)
    compute(1, FAR, 1)
    p_far1 = swap_parts(1, FAR, 1)
    sum_x(1, UP, 2, x_mid1)
    z_mid1 = scatter_z(1, OWN, 3)
    x_far1 = scatter_x(1, FAR, 1, p_far1)
    grad_tiles(0, 4)
    sum_x(1, FAR, 1, x_far1)
    z_far1 = scatter_z(1, FAR, 1)
    grad_tiles(4, 6)
    sum_z(1, OWN, 3, z_mid1)
    sum_z(1, FAR, 1, z_far1)
    y_1 = scatter_y(1)
    grad_tiles(6, 8)
    zg_1 = gather_z(1, y_1)
    grad_tiles(8, 10)
    xg_1 = gather_x(1, zg_1)
    grad_tiles(10, 12)
    for copy in xg_0:
        copy.wait_recv()
    for copy in xg_1:
        copy.wait_recv()
    last = pltpu.make_async_copy(out, out_hbm, load_sem.at[len(loads)])
    last.start()
    for copy in sent:
        copy.wait_send()
    for copy in grad_copies:
        copy.wait()
    last.wait()


N_SEND = 128


def local(out_grad, routes, gate_values, layer_input, w_gate, w_up, w_down):
    any_spec = pl.BlockSpec(memory_space=pl.ANY)
    vmem = pl.BlockSpec(memory_space=pltpu.VMEM)
    return pl.pallas_call(
        kernel,
        out_shape=(
            jax.ShapeDtypeStruct((TOK, D), BF16),
            jax.ShapeDtypeStruct((1, D, U), F32),
            jax.ShapeDtypeStruct((1, D, U), F32),
        ),
        in_specs=[any_spec, vmem, vmem, any_spec, any_spec, any_spec, any_spec],
        out_specs=(any_spec, any_spec, any_spec),
        scratch_shapes=[
            pltpu.VMEM((2, 2, 4, 2, HALF, D), BF16),
            pltpu.VMEM((D, 2 * U), BF16),
            pltpu.VMEM((D, U), BF16),
            pltpu.VMEM((4, 2, EXPERTS, TOK), F32),
            pltpu.VMEM((2, 4, 2, HALF, 2 * U), BF16),
            pltpu.VMEM((2, 4, HALF, D), BF16),
            pltpu.VMEM((2, 4, HALF, D), BF16),
            pltpu.VMEM((2, 4, HALF, D), BF16),
            pltpu.VMEM((3, 2, 4, XROWS, D), BF16),
            pltpu.VMEM((2, 4, XROWS, D), BF16),
            pltpu.VMEM((NZ - 1, 2, 4, XROWS, ZCOLS), BF16),
            pltpu.VMEM((2, 4, XROWS, ZCOLS), BF16),
            pltpu.VMEM((2, 3, XROWS, ZCOLS), BF16),
            pltpu.VMEM((TOK, D), BF16),
            pltpu.VMEM((2, D, U), F32),
            pltpu.SemaphoreType.DMA((8,)),
            pltpu.SemaphoreType.DMA((N_SEND,)),
            pltpu.SemaphoreType.DMA((N_SEND,)),
            pltpu.SemaphoreType.DMA((12,)),
        ],
        compiler_params=pltpu.CompilerParams(
            collective_id=0, has_side_effects=True, vmem_limit_bytes=56 * 2**20
        ),
        cost_estimate=pl.CostEstimate(
            flops=7 * 2 * 1024 * D * U, bytes_accessed=14 * 2**20, transcendentals=1024 * U
        ),
    )(out_grad, routes, gate_values, layer_input, w_gate, w_up, w_down)


def solution(mesh):
    placed = (
        P("expert", None),
        P("expert", None),
        P("expert", None),
        P("expert", None),
        P("expert", None, "dp"),
        P("expert", None, "dp"),
        P("expert", None, "dp"),
    )
    return jax.shard_map(
        local,
        mesh=mesh,
        in_specs=placed,
        out_specs=(P("expert", None), P("expert", None, "dp"), P("expert", None, "dp")),
        check_vma=False,
    )
```

time: 322 us -> 119 us (0.37)
  waiting for transfers between devices: 250 us -> 0 us
  Pallas kernels: 0 us -> 107 us
  matrix products: 32 us -> 0 us
  blocking collectives: 13.3 us -> 0 us
  between operations: 13.8 us -> 0.64 us
    psum x1 -> x0, waiting for transfers between devices: 131 us -> none  [local(): total = lax.psum(total, 'dp')]
    pallas_call x0 -> x1, Pallas kernels: none -> 107 us  [local(): pl.pallas_call(kernel, out_shape=(jax.ShapeDtypeStruct((TOK, D), BF16), j...]
    all_gather x2 -> x0, waiting for transfers between devices: 73.1 us -> none  [the longest x1 39.9 us: local(): grads = lax.all_gather(out_grad, 'expert', axis=0, tiled=True)]
    reduce_scatter x1 -> x0, waiting for transfers between devices: 45.1 us -> none  [local(): lax.psum_scatter(partial.astype(jnp.bfloat16), 'expert', scatter_dimensio...]
    dot_general x7 -> x0, matrix products: 32 us -> none  [the longest x1 6.32 us: local(): grad_gate = jnp.dot(rows.T, gate_grad, preferred_element_type=jnp.float32)]
    all_gather x1 -> x0, blocking collectives: 13.3 us -> none  [local(): weight = lax.all_gather(dense, 'expert', axis=0, tiled=True)]
    unnamed x11 -> x7, local copies, waits for them, and re-layouts: 9.69 us -> 10.5 us
  transfers between devices with their start and end apart: 4 -> 0, of which waited for: 4 -> 0; matrix products, arithmetic and copies ran while one was open for 8% -> 0% of each run, Pallas kernels for 0% -> 0%
where the time goes in v2:
time: 119 us; the launch traced here: 118 us
  Pallas kernels  107 us (90%)
  local copies, waits for them, and re-layouts  10.5 us (9%)
    pallas_call x1, Pallas kernels, local(): pl.pallas_call(kernel, out_shape=(jax.ShapeDtypeStruct((TOK, D), BF16), j...  107 us
    unnamed x7, local copies, waits for them, and re-layouts  10.5 us

profile of v2, /device:TPU:32, one launch (start us, length us, event | category | flops | bytes accessed | tf_op | source)
XLA Modules:
  0.0 118.5 jit_solution(3514928113054223148)
XLA Ops:
  0.6 1.4 %copy.10.routes_in = s32[128,4]{1,0:T(8,128)} copy(s32[128,4]{0,1:T(4,128)} %param.8) | data formatting | bytes 4096 | tf_op args[1]
  2.0 1.4 %copy.11.gates_in = f32[128,4]{1,0:T(8,128)} copy(f32[128,4]{0,1:T(4,128)} %param.9) | data formatting | bytes 4096 | tf_op args[2]
  3.5 107.3 %shard_map.94 = (bf16[128,3072]{1,0:T(8,128)(2,1)}, f32[1,3072,256]{2,1,0:T(8,128)}, f32[1,3072,256]{2,1,0:T(8,128)}) custom-call(bf16[128,3072]{1,0:T(8,128)(2,1)} %og_in.1, s32[128,4]{1,0:T(8,128)} %copy.10.routes_in, f32[128,4]{1,0:T(8,128)} %copy.11.gates_in, bf16[128,3072]{1,0:T(8,128)(2,1)} %x_in.1, bf16[1,3072,256]{2,1,0:T(8,128)(2,1)} %wg_in.1, ...), custom_call_target="tpu_custom_call" | custom-call | flops 11274289152 | bytes 14680064 | tf_op jit(solution)/shard_map/pallas_call | solution.py:339
  110.8 2.1 %copy.15 = bf16[128,3072]{1,0:T(8,128)(2,1)} copy(bf16[128,3072]{1,0:T(8,128)(2,1)} %get-tuple-element.6) | data formatting | bytes 1572864
  112.9 0.0 copy-start
  112.9 3.9 %copy.16 = f32[1,3072,256]{2,1,0:T(8,128)} copy(f32[1,3072,256]{2,1,0:T(8,128)} %get-tuple-element.7) | data formatting | bytes 6291456
  116.8 0.0 copy-done
  116.8 1.7 %copy.17 = f32[1,3072,256]{2,1,0:T(8,128)} copy(f32[1,3072,256]{2,1,0:T(8,128)S(1)} %copy-done) | data formatting | bytes 6291456
Async XLA Ops:
  112.9 3.9 %copy-start = (f32[1,3072,256]{2,1,0:T(8,128)S(1)}, f32[1,3072,256]{2,1,0:T(8,128)}, u32[]{:S(2)}) copy-start(f32[1,3072,256]{2,1,0:T(8,128)} %get-tuple-element.8) | copy-start | bytes 9437188

commit v3 on v2

v3 whole, which is shorter than its diff:
```python
import functools

import jax
import jax.numpy as jnp
from jax import lax
from jax.experimental import pallas as pl
from jax.experimental.pallas import tpu as pltpu
from jax.sharding import PartitionSpec as P

MESH = pl.DeviceIdType.MESH
BF16, F32 = jnp.bfloat16, jnp.float32
EXPERTS = 8
NX, NY, NZ = 4, 4, 8
TOK, D, U = 128, 3072, 256
HALF = TOK // 2
XROWS = HALF // NX
ZCOLS = D // NZ
OWN, UP, DOWN, FAR = 0, 1, 2, 3
TO_Y = ((FAR, 2), (DOWN, 1), (UP, 3))
NEAR = ((DOWN, 1), (UP, 3))
TILE = 256


def kernel(
    og_in, routes_in, gates_in, x_in, wg_in, wu_in, wd_in,
    out, gg, gu,
    xo, wgu, wd, g8, dg, ps, pr, s, xr, u, zr, v, yr,
    load_sem, send_sem, recv_sem,
):
    dp, ex = lax.axis_index("dp"), lax.axis_index("expert")
    x, z = lax.rem(dp, NX), lax.div(dp, NX)
    y, c = lax.div(ex, 2), lax.rem(ex, 2)

    def dev(nx, ny, nz, nc):
        return (nz * NX + nx, ny * 2 + nc)

    sib = dev(x, y, z, 1 - c)
    y_at = {d: lax.rem(y + d, NY) for d in (1, 2, 3)}
    x_at = {d: lax.rem(x + d, NX) for d in (1, 2, 3)}
    z_at = {d: lax.rem(z + d, NZ) for d in range(1, NZ)}
    to_y = {d: dev(x, y_at[d], z, c) for d in y_at}
    to_x = {d: dev(x_at[d], y, z, c) for d in x_at}
    to_z = {d: dev(x, y, z_at[d], c) for d in z_at}

    loads = []

    def load(src, dst):
        copy = pltpu.make_async_copy(src, dst, load_sem.at[len(loads)])
        copy.start()
        loads.append(copy)
        return copy

    sent = []

    def send(src, dst, device):
        i = len(sent)
        copy = pltpu.make_async_remote_copy(
            src_ref=src, dst_ref=dst, send_sem=send_sem.at[i], recv_sem=recv_sem.at[i],
            device_id=device, device_id_type=MESH,
        )
        copy.start()
        sent.append(copy)
        return copy

    own_loads = {}
    for h in range(2):
        for a, ref in ((0, x_in), (1, og_in)):
            own_loads[a, h] = load(ref.at[pl.ds(h * HALF, HALF)], xo.at[a, h, OWN, 0])
    weight_loads = [
        load(wg_in.at[0], wgu.at[:, pl.ds(0, U)]),
        load(wu_in.at[0], wgu.at[:, pl.ds(U, U)]),
        load(wd_in.at[0], wd),
    ]

    peers = [sib] + list(to_y.values()) + list(to_x.values()) + list(to_z.values())
    barrier = pltpu.get_barrier_semaphore()
    for device in peers:
        pl.semaphore_signal(barrier, inc=1, device_id=device, device_id_type=MESH)

    lane = lax.broadcasted_iota(jnp.int32, (TOK, TOK), 1)
    row = lax.broadcasted_iota(jnp.int32, (TOK, TOK), 0)
    for e in range(EXPERTS):
        g8[OWN, 0, e : e + 1, :] = jnp.sum(
            jnp.where(routes_in[...] == e, gates_in[...], 0.0), axis=0, keepdims=True
        )

    pl.semaphore_wait(barrier, len(peers))

    g_move = {j: send(g8.at[OWN, 0], g8.at[j, 0], to_y[d]) for j, d in TO_Y}
    g_swap = {OWN: send(g8.at[OWN, 0], g8.at[OWN, 1], sib)}
    swap = {}
    x_cols = pl.ds(pl.multiple_of(x * (D // NX), D // NX), D // NX)
    z_cols = pl.ds(pl.multiple_of(z * ZCOLS, ZCOLS), ZCOLS)

    def groups(first, count):
        return pl.ds(first * 16, count * 16)

    NEAR_D, NEAR_X, FAR_X, FAR_Z = 3, 1, 2, 2
    near_d, near_x = groups(0, NEAR_D), groups(NEAR_D, NEAR_X)
    far_x, far_z = groups(0, FAR_X), groups(FAR_X, FAR_Z)

    def move(h, j, rows, cols, device):
        piece = xo.at[:, h, OWN, 0, rows, cols]
        return send(piece, xo.at[:, h, j, 0, rows, cols], device)

    def do_swap(h, j, rows):
        swap.setdefault((h, j), []).append(send(xo.at[:, h, j, 0, rows], xo.at[:, h, j, 1, rows], sib))

    def send_small(h):
        far = [move(h, FAR, far_z, z_cols, to_y[2]), move(h, FAR, far_x, x_cols, to_y[2])]
        near = [move(h, j, near_x, x_cols, to_y[d]) for j, d in NEAR]
        return far, near

    def send_direct(h):
        return [move(h, j, near_d, slice(None), to_y[d]) for j, d in NEAR]

    def share(h, small):
        far, near = small
        for copy in far:
            copy.wait_recv()
        far_got = []
        for d in (4, 3, 5, 2, 6, 1, 7):
            piece = xo.at[:, h, FAR, 0, far_z, z_cols]
            far_got.append(send(piece, piece, to_z[d]))
        for d in (2, 1, 3):
            piece = xo.at[:, h, FAR, 0, far_x, x_cols]
            far_got.append(send(piece, piece, to_x[d]))
        for copy in near:
            copy.wait_recv()
        near_got = []
        for d in (2, 1, 3):
            piece = xo.at[:, h, pl.ds(UP, 2), 0, near_x, x_cols]
            near_got.append(send(piece, piece, to_x[d]))
        return far_got, near_got

    def far_arrive(h, got):
        for copy in got:
            copy.wait_recv()
        do_swap(h, FAR, groups(0, 4))

    def direct_arrive(h, got):
        for copy in got:
            copy.wait_recv()

    def direct_swap(h):
        for j, _ in NEAR:
            do_swap(h, j, near_d)

    def shared_arrive(h, got):
        for copy in got:
            copy.wait_recv()
        for j, _ in NEAR:
            do_swap(h, j, near_x)

    for a in range(2):
        own_loads[a, 0].wait()
    small_0 = send_small(0)
    direct_0 = send_direct(0)
    do_swap(0, OWN, groups(0, 4))
    for a in range(2):
        own_loads[a, 1].wait()
    do_swap(1, OWN, groups(0, 4))

    def weight_column(h, j, slot):
        mine = lax.broadcasted_iota(jnp.int32, (EXPERTS, TOK), 0) == ex
        line = jnp.sum(jnp.where(mine, g8[j, slot], 0.0), axis=0, keepdims=True)
        whole = jnp.sum(jnp.where(lane == row, line, 0.0), axis=1, keepdims=True)
        return whole[h * HALF : (h + 1) * HALF]

    def compute(h, j, n):
        rows = n * TOK
        for jj in range(j, j + n):
            for copy in swap[h, jj]:
                copy.wait_recv()
        weight = jnp.concatenate(
            [weight_column(h, jj, slot) for jj in range(j, j + n) for slot in range(2)], axis=0
        )
        tokens = xo[0, h, j : j + n].reshape(rows, D)
        gate_pre = jnp.dot(tokens, wgu[:, :U], preferred_element_type=F32)
        up_pre = jnp.dot(tokens, wgu[:, U:], preferred_element_type=F32)
        grads_in = xo[1, h, j : j + n].reshape(rows, D)
        hidden = weight * jnp.dot(grads_in, wd[...], preferred_element_type=F32)
        sig = jax.nn.sigmoid(gate_pre)
        up_grad = (hidden * (gate_pre * sig)).astype(BF16)
        gate_grad = (hidden * up_pre * sig * (1.0 + gate_pre * (1.0 - sig))).astype(BF16)
        both = jnp.concatenate([gate_grad, up_grad], axis=1)
        dg[h, j : j + n] = both.reshape(n, 2, HALF, 2 * U)

        def tile(i, carry):
            cols = pl.ds(pl.multiple_of(i * TILE, TILE), TILE)
            part = lax.dot_general(
                dg[h, j : j + n].reshape(rows, 2 * U), wgu[cols, :], (((1,), (1,)), ((), ())),
                preferred_element_type=F32,
            ).astype(BF16).reshape(n, 2, HALF, TILE)
            s[h, j : j + n, :, cols] = part[:, 0]
            ps[h, j : j + n, :, cols] = part[:, 1]
            return carry

        lax.fori_loop(0, D // TILE, tile, 0)

    def swap_parts(h, j, n):
        return send(ps.at[h, pl.ds(j, n)], pr.at[h, pl.ds(j, n)], sib)

    def scatter_x(h, j, n, swapped):
        swapped.wait_recv()
        for jj in range(j, j + n):
            s[h, jj] = (s[h, jj].astype(F32) + pr[h, jj].astype(F32)).astype(BF16)
        got = []
        for d in (1, 3, 2):
            rows = pl.ds(pl.multiple_of(x_at[d] * XROWS, XROWS), XROWS)
            got.append(
                send(s.at[h, pl.ds(j, n), rows], xr.at[d - 1, h, pl.ds(j, n)], to_x[d])
            )
        return got

    y_got = {0: [], 1: []}
    y_dist = {UP: 1, DOWN: 3, FAR: 2}

    def sum_x(h, j, n, got):
        for copy in got:
            copy.wait_recv()
        rows = pl.ds(pl.multiple_of(x * XROWS, XROWS), XROWS)
        for jj in range(j, j + n):
            total = s[h, jj, rows].astype(F32)
            for d in range(3):
                total = total + xr[d, h, jj].astype(F32)
            u[h, jj] = total.astype(BF16)
            if jj != OWN:
                y_got[h].append(send(u.at[h, jj], yr.at[h, jj - 1], to_y[y_dist[jj]]))

    def scatter_z(h):
        for copy in y_got[h]:
            copy.wait_recv()
        total = u[h, OWN].astype(F32)
        for j in range(3):
            total = total + yr[h, j].astype(F32)
        v[h] = total.astype(BF16)
        got = []
        for d in (4, 3, 5, 2, 6, 1, 7):
            cols = pl.ds(pl.multiple_of(z_at[d] * ZCOLS, ZCOLS), ZCOLS)
            got.append(send(v.at[h, :, cols], zr.at[d - 1, h], to_z[d]))
        return got

    def place(h):
        return pl.ds(pl.multiple_of(h * HALF + x * XROWS, XROWS), XROWS)

    def gather_z(h, got):
        for copy in got:
            copy.wait_recv()
        total = v[h, :, z_cols].astype(F32)
        for d in range(NZ - 1):
            total = total + zr[d, h].astype(F32)
        out[place(h), z_cols] = total.astype(BF16)
        piece = out.at[place(h), z_cols]
        return [send(piece, piece, to_z[d]) for d in (4, 3, 5, 2, 6, 1, 7)]

    def gather_x(h, got):
        for copy in got:
            copy.wait_recv()
        piece = out.at[place(h)]
        return [send(piece, piece, to_x[d]) for d in (1, 3, 2)]

    def grad_tiles(first, last):
        def tile(i, carry):
            cols = pl.ds(pl.multiple_of(i * TILE, TILE), TILE)
            part = lax.dot_general(
                xo[0, :, :, :, :, cols].reshape(8 * TOK, TILE),
                dg[...].reshape(8 * TOK, 2 * U),
                (((0,), (0,)), ((), ())),
                preferred_element_type=F32,
            )
            gg[0, cols] = part[:, :U]
            gu[0, cols] = part[:, U:]
            return carry

        lax.fori_loop(first, last, tile, 0)

    g_swap[OWN].wait_recv()
    for copy in weight_loads:
        copy.wait()
    compute(0, OWN, 1)
    p_own0 = swap_parts(0, OWN, 1)
    far_0, near_0 = share(0, small_0)
    small_1 = send_small(1)
    compute(1, OWN, 1)
    p_own1 = swap_parts(1, OWN, 1)
    for j, _ in TO_Y:
        g_move[j].wait_recv()
        g_swap[j] = send(g8.at[j, 0], g8.at[j, 1], sib)
    x_own0 = scatter_x(0, OWN, 1, p_own0)
    x_own1 = scatter_x(1, OWN, 1, p_own1)
    for j, _ in TO_Y:
        g_swap[j].wait_recv()
    direct_arrive(0, direct_0)
    direct_1 = send_direct(1)
    direct_swap(0)
    far_1, near_1 = share(1, small_1)
    shared_arrive(0, near_0)
    compute(0, UP, 2)
    p_near0 = swap_parts(0, UP, 2)
    far_arrive(0, far_0)
    sum_x(0, OWN, 1, x_own0)
    x_near0 = scatter_x(0, UP, 2, p_near0)
    compute(0, FAR, 1)
    p_far0 = swap_parts(0, FAR, 1)
    sum_x(1, OWN, 1, x_own1)
    x_far0 = scatter_x(0, FAR, 1, p_far0)
    far_arrive(1, far_1)
    sum_x(0, UP, 2, x_near0)
    compute(1, FAR, 1)
    p_far1 = swap_parts(1, FAR, 1)
    sum_x(0, FAR, 1, x_far0)
    x_far1 = scatter_x(1, FAR, 1, p_far1)
    direct_arrive(1, direct_1)
    direct_swap(1)
    shared_arrive(1, near_1)
    z_0 = scatter_z(0)
    compute(1, UP, 1)
    p_up1 = swap_parts(1, UP, 1)
    compute(1, DOWN, 1)
    p_down1 = swap_parts(1, DOWN, 1)
    x_up1 = scatter_x(1, UP, 1, p_up1)
    x_down1 = scatter_x(1, DOWN, 1, p_down1)
    zg_0 = gather_z(0, z_0)
    sum_x(1, FAR, 1, x_far1)
    grad_tiles(0, 2)
    xg_0 = gather_x(0, zg_0)
    grad_tiles(2, 4)
    sum_x(1, UP, 1, x_up1)
    sum_x(1, DOWN, 1, x_down1)
    grad_tiles(4, 6)
    z_1 = scatter_z(1)
    grad_tiles(6, 8)
    zg_1 = gather_z(1, z_1)
    grad_tiles(8, 10)
    xg_1 = gather_x(1, zg_1)
    grad_tiles(10, 12)
    for copy in xg_0 + xg_1:
        copy.wait_recv()
    for copy in sent:
        copy.wait_send()


N_SEND = 128


def local(out_grad, routes, gate_values, layer_input, w_gate, w_up, w_down):
    any_spec = pl.BlockSpec(memory_space=pl.ANY)
    vmem = pl.BlockSpec(memory_space=pltpu.VMEM)
    return pl.pallas_call(
        kernel,
        out_shape=(
            pltpu.VMEM((TOK, D), BF16),
            pltpu.VMEM((1, D, U), F32),
            pltpu.VMEM((1, D, U), F32),
        ),
        in_specs=[any_spec, vmem, vmem, any_spec, any_spec, any_spec, any_spec],
        out_specs=(vmem, vmem, vmem),
        scratch_shapes=[
            pltpu.VMEM((2, 2, 4, 2, HALF, D), BF16),
            pltpu.VMEM((D, 2 * U), BF16),
            pltpu.VMEM((D, U), BF16),
            pltpu.VMEM((4, 2, EXPERTS, TOK), F32),
            pltpu.VMEM((2, 4, 2, HALF, 2 * U), BF16),
            pltpu.VMEM((2, 4, HALF, D), BF16),
            pltpu.VMEM((2, 4, HALF, D), BF16),
            pltpu.VMEM((2, 4, HALF, D), BF16),
            pltpu.VMEM((3, 2, 4, XROWS, D), BF16),
            pltpu.VMEM((2, 4, XROWS, D), BF16),
            pltpu.VMEM((NZ - 1, 2, XROWS, ZCOLS), BF16),
            pltpu.VMEM((2, XROWS, D), BF16),
            pltpu.VMEM((2, 3, XROWS, D), BF16),
            pltpu.SemaphoreType.DMA((8,)),
            pltpu.SemaphoreType.DMA((N_SEND,)),
            pltpu.SemaphoreType.DMA((N_SEND,)),
        ],
        compiler_params=pltpu.CompilerParams(
            collective_id=0, has_side_effects=True, vmem_limit_bytes=56 * 2**20
        ),
        cost_estimate=pl.CostEstimate(
            flops=7 * 2 * 1024 * D * U, bytes_accessed=14 * 2**20, transcendentals=1024 * U
        ),
    )(out_grad, routes.T, gate_values.T, layer_input, w_gate, w_up, w_down)


def solution(mesh):
    placed = (
        P("expert", None),
        P("expert", None),
        P("expert", None),
        P("expert", None),
        P("expert", None, "dp"),
        P("expert", None, "dp"),
        P("expert", None, "dp"),
    )
    return jax.shard_map(
        local,
        mesh=mesh,
        in_specs=placed,
        out_specs=(P("expert", None), P("expert", None, "dp"), P("expert", None, "dp")),
        check_vma=False,
    )
```

time: 119 us -> 107 us (0.90)
  local copies, waits for them, and re-layouts: 10.5 us -> 4.21 us
  Pallas kernels: 107 us -> 101 us
    unnamed x7 -> x3, local copies, waits for them, and re-layouts: 10.5 us -> 4.21 us
    pallas_call x1, Pallas kernels: 107 us -> 101 us  [local(): pl.pallas_call(kernel, out_shape=(pltpu.VMEM((TOK, D), BF16), pltpu.VMEM(...]
where the time goes in v3:
time: 107 us; the launch traced here: 106 us
  Pallas kernels  101 us (94%)
  local copies, waits for them, and re-layouts  4.21 us (4%)
    pallas_call x1, Pallas kernels, local(): pl.pallas_call(kernel, out_shape=(pltpu.VMEM((TOK, D), BF16), pltpu.VMEM(...  101 us
    unnamed x3, local copies, waits for them, and re-layouts  4.21 us

profile of v3, /device:TPU:32, one launch (start us, length us, event | category | flops | bytes accessed | tf_op | source)
XLA Modules:
  0.0 106.1 jit_solution(7316838111626720544)
XLA Ops:
  0.6 101.3 %shard_map.94 = (bf16[128,3072]{1,0:T(8,128)(2,1)S(1)}, f32[1,3072,256]{2,1,0:T(8,128)S(1)}, f32[1,3072,256]{2,1,0:T(8,128)S(1)}) custom-call(bf16[128,3072]{1,0:T(8,128)(2,1)} %og_in.1, s32[4,128]{1,0:T(4,128)} %bitcast.2, f32[4,128]{1,0:T(4,128)} %bitcast.3, bf16[128,3072]{1,0:T(8,128)(2,1)} %x_in.1, bf16[1,3072,256]{2,1,0:T(8,128)(2,1)} %wg_in.1, ...), custom_call_target="tpu_custom_call" | custom-call | flops 11274289152 | bytes 14680064 | tf_op jit(solution)/shard_map/pallas_call | solution.py:350
  101.9 0.9 copy.13
  102.8 1.7 %copy.14 = f32[1,3072,256]{2,1,0:T(8,128)} copy(f32[1,3072,256]{2,1,0:T(8,128)S(1)} %get-tuple-element.4) | data formatting | bytes 6291456
  104.5 1.7 %copy.15 = f32[1,3072,256]{2,1,0:T(8,128)} copy(f32[1,3072,256]{2,1,0:T(8,128)S(1)} %get-tuple-element.5) | data formatting | bytes 6291456

commit v4 on v3

v4 whole, which is shorter than its diff:
```python
import functools

import jax
import jax.numpy as jnp
from jax import lax
from jax.experimental import pallas as pl
from jax.experimental.pallas import tpu as pltpu
from jax.sharding import PartitionSpec as P

MESH = pl.DeviceIdType.MESH
BF16, F32 = jnp.bfloat16, jnp.float32
EXPERTS = 8
NX, NY, NZ = 4, 4, 8
TOK, D, U = 128, 3072, 256
HALF = TOK // 2
XCOLS = D // NX
ZROWS = 16
ZCOLS = XCOLS // 2
FAR_COLS = D // NZ
OWN, UP, DOWN, FAR = 0, 1, 2, 3
TO_Y = ((FAR, 2), (DOWN, 1), (UP, 3))
NEAR = ((DOWN, 1), (UP, 3))
TILE, BACK, TURN = 256, 1536, 512
X_ORDER, Z_ORDER = (2, 1, 3), (4, 3, 5, 2, 6, 1, 7)
NEAR_X, FAR_X = 1, 1


def kernel(
    og_in, routes_in, gates_in, x_in, wg_in, wu_in, wd_in,
    out, gg, gu,
    xo, wgu, wgu_t, wd, g8, dg, ps, pr, s, xr, u, zr, v, yr, yf,
    load_sem, send_sem, recv_sem,
):
    dp, ex = lax.axis_index("dp"), lax.axis_index("expert")
    x, z = lax.rem(dp, NX), lax.div(dp, NX)
    y, c = lax.div(ex, 2), lax.rem(ex, 2)

    def dev(nx, ny, nz, nc):
        return (nz * NX + nx, ny * 2 + nc)

    sib = dev(x, y, z, 1 - c)
    y_at = {d: lax.rem(y + d, NY) for d in (1, 2, 3)}
    x_at = {d: lax.rem(x + d, NX) for d in (1, 2, 3)}
    z_at = {d: lax.rem(z + d, NZ) for d in range(1, NZ)}
    to_y = {d: dev(x, y_at[d], z, c) for d in y_at}
    to_x = {d: dev(x_at[d], y, z, c) for d in x_at}
    to_z = {d: dev(x, y, z_at[d], c) for d in z_at}

    loads = []

    def load(src, dst):
        assert len(loads) < 8
        copy = pltpu.make_async_copy(src, dst, load_sem.at[len(loads)])
        copy.start()
        loads.append(copy)
        return copy

    sent = []

    def send(src, dst, device):
        i = len(sent)
        assert i < N_SEND
        copy = pltpu.make_async_remote_copy(
            src_ref=src, dst_ref=dst, send_sem=send_sem.at[i], recv_sem=recv_sem.at[i],
            device_id=device, device_id_type=MESH,
        )
        copy.start()
        sent.append(copy)
        return copy

    own_loads = {}
    for h in range(2):
        for a, ref in ((0, x_in), (1, og_in)):
            own_loads[a, h] = load(ref.at[pl.ds(h * HALF, HALF)], xo.at[a, h, OWN, 0])
    weight_loads = [
        load(wg_in.at[0], wgu.at[:, pl.ds(0, U)]),
        load(wu_in.at[0], wgu.at[:, pl.ds(U, U)]),
        load(wd_in.at[0], wd),
    ]

    peers = [sib] + list(to_y.values()) + list(to_x.values()) + list(to_z.values())
    barrier = pltpu.get_barrier_semaphore()
    for device in peers:
        pl.semaphore_signal(barrier, inc=1, device_id=device, device_id_type=MESH)

    lane = lax.broadcasted_iota(jnp.int32, (TOK, TOK), 1)
    row = lax.broadcasted_iota(jnp.int32, (TOK, TOK), 0)
    for e in range(EXPERTS):
        g8[OWN, 0, e : e + 1, :] = jnp.sum(
            jnp.where(routes_in[...] == e, gates_in[...], 0.0), axis=0, keepdims=True
        )

    pl.semaphore_wait(barrier, len(peers))

    g_move = {j: send(g8.at[OWN, 0], g8.at[j, 0], to_y[d]) for j, d in TO_Y}
    g_swap = {OWN: send(g8.at[OWN, 0], g8.at[OWN, 1], sib)}
    x_cols = pl.ds(pl.multiple_of(x * XCOLS, XCOLS), XCOLS)
    z_cols = pl.ds(pl.multiple_of(z * FAR_COLS, FAR_COLS), FAR_COLS)

    def groups(first, count):
        return pl.ds(first * 16, count * 16)

    near_x = groups(4 - NEAR_X, NEAR_X)
    far_x, far_z = groups(0, FAR_X), groups(FAR_X, 4 - FAR_X)

    def move(h, j, rows, cols, device):
        piece = xo.at[:, h, OWN, 0, rows, cols]
        return send(piece, xo.at[:, h, j, 0, rows, cols], device)

    swap, swapped = {}, set()

    def do_swap(h, j, first, count):
        rows = groups(first, count)
        copy = send(xo.at[:, h, j, 0, rows], xo.at[:, h, j, 1, rows], sib)
        for g in range(first, first + count):
            swap[h, j, g] = copy

    def swap_wait(h, j, first, count):
        for g in range(first, first + count):
            if id(swap[h, j, g]) not in swapped:
                swapped.add(id(swap[h, j, g]))
                swap[h, j, g].wait_recv()

    def wait_all(copies):
        for copy in copies:
            copy.wait_recv()

    def send_small(h):
        far = []
        if FAR_X < 4:
            far.append(move(h, FAR, far_z, z_cols, to_y[2]))
        if FAR_X:
            far.append(move(h, FAR, far_x, x_cols, to_y[2]))
        near = [move(h, j, near_x, x_cols, to_y[d]) for j, d in NEAR if NEAR_X]
        return far, near

    def send_direct(h, first, count):
        return [move(h, j, groups(first, count), slice(None), to_y[d]) for j, d in NEAR]

    def share(h, small):
        far, near = small
        wait_all(far)
        far_got, near_got = [], []
        for d in Z_ORDER if FAR_X < 4 else ():
            piece = xo.at[:, h, FAR, 0, far_z, z_cols]
            far_got.append(send(piece, piece, to_z[d]))
        for d in X_ORDER:
            if FAR_X:
                piece = xo.at[:, h, FAR, 0, far_x, x_cols]
                far_got.append(send(piece, piece, to_x[d]))
        wait_all(near)
        for d in X_ORDER:
            if NEAR_X:
                piece = xo.at[:, h, pl.ds(UP, 2), 0, near_x, x_cols]
                near_got.append(send(piece, piece, to_x[d]))
        return far_got, near_got

    def far_arrive(h, got):
        wait_all(got)
        do_swap(h, FAR, 0, 4)

    def near_arrive(h, got, first, count):
        wait_all(got)
        for j, _ in NEAR:
            do_swap(h, j, first, count)

    for a in range(2):
        own_loads[a, 0].wait()
    small_0 = send_small(0)
    for a in range(2):
        own_loads[a, 1].wait()
    small_1 = send_small(1)
    first_0 = send_direct(0, 0, 2)
    second_0 = send_direct(0, 2, 2 - NEAR_X)
    do_swap(0, OWN, 0, 4)
    do_swap(1, OWN, 0, 4)

    def weight_column(h, j, slot, first, count):
        mine = lax.broadcasted_iota(jnp.int32, (EXPERTS, TOK), 0) == ex
        line = jnp.sum(jnp.where(mine, g8[j, slot], 0.0), axis=0, keepdims=True)
        whole = jnp.sum(jnp.where(lane == row, line, 0.0), axis=1, keepdims=True)
        start = h * HALF + first * 16
        return whole[start : start + count * 16]

    def compute(h, j, n, first, count):
        rows, sub = n * 2 * count * 16, groups(first, count)
        for jj in range(j, j + n):
            swap_wait(h, jj, first, count)
        weight = jnp.concatenate(
            [weight_column(h, jj, slot, first, count) for jj in range(j, j + n) for slot in range(2)],
            axis=0,
        )
        tokens = xo[0, h, j : j + n, :, sub].reshape(rows, D)
        gate_pre = jnp.dot(tokens, wgu[:, :U], preferred_element_type=F32)
        up_pre = jnp.dot(tokens, wgu[:, U:], preferred_element_type=F32)
        grads_in = xo[1, h, j : j + n, :, sub].reshape(rows, D)
        hidden = weight * jnp.dot(grads_in, wd[...], preferred_element_type=F32)
        sig = jax.nn.sigmoid(gate_pre)
        up_grad = (hidden * (gate_pre * sig)).astype(BF16)
        gate_grad = (hidden * up_pre * sig * (1.0 + gate_pre * (1.0 - sig))).astype(BF16)
        both = jnp.concatenate([gate_grad, up_grad], axis=1)
        dg[h, j : j + n, :, sub] = both.reshape(n, 2, count * 16, 2 * U)

        def tile(i, carry):
            cols = pl.ds(pl.multiple_of(i * BACK, BACK), BACK)
            part = jnp.dot(both, wgu_t[:, cols], preferred_element_type=F32)
            part = part.astype(BF16).reshape(n, 2, count * 16, BACK)
            s[h, j : j + n, sub, cols] = part[:, 0]
            ps[h, j : j + n, sub, cols] = part[:, 1]
            return carry

        lax.fori_loop(0, D // BACK, tile, 0)
        piece = (h, pl.ds(j, n), sub)
        return send(ps.at[piece], pr.at[piece], sib)

    def merge(h, j, n, first, count, parts):
        sub = groups(first, count)
        parts.wait_recv()
        for jj in range(j, j + n):
            s[h, jj, sub] = (s[h, jj, sub].astype(F32) + pr[h, jj, sub].astype(F32)).astype(BF16)

    def send_x(h, j, n, first, count):
        sub = groups(first, count)
        got = []
        for d in X_ORDER:
            cols = pl.ds(pl.multiple_of(x_at[d] * XCOLS, XCOLS), XCOLS)
            got.append(
                send(s.at[h, pl.ds(j, n), sub, cols], xr.at[d - 1, h, pl.ds(j, n), sub], to_x[d])
            )
        return got

    def scatter_x(h, j, n, first, count, parts):
        merge(h, j, n, first, count, parts)
        return send_x(h, j, n, first, count)

    def scatter_near(h, j, n, first, count, parts):
        merge(h, j, n, first, count, parts)
        sub = groups(first, count)
        return [
            send(s.at[h, UP, sub], yf.at[0, sub], to_y[1]),
            send(s.at[h, DOWN, sub], yf.at[1, sub], to_y[3]),
        ]

    def sum_near(h, j, n, first, count, got):
        wait_all(got)
        sub = groups(first, count)
        total = s[h, OWN, sub].astype(F32) + yf[0, sub].astype(F32) + yf[1, sub].astype(F32)
        s[h, OWN, sub] = total.astype(BF16)
        return send_x(h, OWN, 1, first, count)

    y_got = {0: [], 1: []}
    y_dist = {UP: 1, DOWN: 3, FAR: 2}

    def sum_x(h, j, n, first, count, got):
        sub = groups(first, count)
        wait_all(got)
        for jj in range(j, j + n):
            total = s[h, jj, sub, x_cols].astype(F32)
            for d in range(3):
                total = total + xr[d, h, jj, sub].astype(F32)
            u[h, jj, sub] = total.astype(BF16)
            if jj != OWN:
                y_got[h].append(send(u.at[h, jj, sub], yr.at[h, jj - 1, sub], to_y[y_dist[jj]]))

    def z_part(nz):
        rows = pl.ds(pl.multiple_of(lax.rem(nz, 4) * ZROWS, ZROWS), ZROWS)
        return rows, pl.ds(pl.multiple_of(lax.div(nz, 4) * ZCOLS, ZCOLS), ZCOLS)

    def scatter_z(h):
        wait_all(y_got[h])
        total = u[h, OWN].astype(F32)
        for j in range(3) if h == 0 else (FAR - 1,):
            total = total + yr[h, j].astype(F32)
        v[h] = total.astype(BF16)
        got = []
        for d in Z_ORDER:
            rows, cols = z_part(z_at[d])
            got.append(send(v.at[h, rows, cols], zr.at[d - 1, h], to_z[d]))
        return got

    def gather_z(h, got):
        wait_all(got)
        rows, cols = z_part(z)
        total = v[h, rows, cols].astype(F32)
        for d in range(NZ - 1):
            total = total + zr[d, h].astype(F32)
        rows = pl.ds(pl.multiple_of(h * HALF + lax.rem(z, 4) * ZROWS, ZROWS), ZROWS)
        cols = pl.ds(pl.multiple_of(x * XCOLS + lax.div(z, 4) * ZCOLS, ZCOLS), ZCOLS)
        out[rows, cols] = total.astype(BF16)
        piece = out.at[rows, cols]
        return [send(piece, piece, to_z[d]) for d in Z_ORDER]

    def gather_x(h, got):
        wait_all(got)
        piece = out.at[pl.ds(h * HALF, HALF), x_cols]
        return [send(piece, piece, to_x[d]) for d in X_ORDER]

    def grad_tiles(first, last):
        def tile(i, carry):
            cols = pl.ds(pl.multiple_of(i * TILE, TILE), TILE)
            part = lax.dot_general(
                xo[0, :, :, :, :, cols].reshape(8 * TOK, TILE),
                dg[...].reshape(8 * TOK, 2 * U),
                (((0,), (0,)), ((), ())),
                preferred_element_type=F32,
            )
            gg[0, cols] = part[:, :U]
            gu[0, cols] = part[:, U:]
            return carry

        lax.fori_loop(first, last, tile, 0)

    own0, own1 = (0, OWN, 1, 0, 4), (1, OWN, 1, 0, 4)
    near0, far0, far1 = (0, UP, 2, 0, 4), (0, FAR, 1, 0, 4), (1, FAR, 1, 0, 4)
    first1, second1 = (1, UP, 2, 0, 2), (1, UP, 2, 2, 2)

    for copy in weight_loads:
        copy.wait()

    def turn(i, carry):
        cols = pl.ds(pl.multiple_of(i * TURN, TURN), TURN)
        wgu_t[:, cols] = wgu[cols, :].T
        return carry

    lax.fori_loop(0, D // TURN, turn, 0)
    g_swap[OWN].wait_recv()
    p_own0 = compute(*own0)
    far_0, shared_0 = share(0, small_0)
    far_1, shared_1 = share(1, small_1)
    p_own1 = compute(*own1)
    for j, _ in TO_Y:
        g_move[j].wait_recv()
        g_swap[j] = send(g8.at[j, 0], g8.at[j, 1], sib)
    x_own0 = scatter_x(*own0, p_own0)
    merge(*own1, p_own1)
    near_arrive(0, first_0, 0, 2)
    first_1 = send_direct(1, 0, 2)
    near_arrive(0, second_0, 2, 2 - NEAR_X)
    second_1 = send_direct(1, 2, 2 - NEAR_X)
    if NEAR_X:
        near_arrive(0, shared_0, 4 - NEAR_X, NEAR_X)
    for j, _ in TO_Y:
        g_swap[j].wait_recv()
    p_near0 = compute(*near0)
    sum_x(*own0, x_own0)
    x_near0 = scatter_x(*near0, p_near0)
    far_arrive(0, far_0)
    p_far0 = compute(*far0)
    near_arrive(1, first_1, 0, 2)
    x_far0 = scatter_x(*far0, p_far0)
    p_first1 = compute(*first1)
    far_arrive(1, far_1)
    y_first1 = scatter_near(*first1, p_first1)
    sum_x(*near0, x_near0)
    p_far1 = compute(*far1)
    near_arrive(1, second_1, 2, 2 - NEAR_X)
    if NEAR_X:
        near_arrive(1, shared_1, 4 - NEAR_X, NEAR_X)
    x_far1 = scatter_x(*far1, p_far1)
    p_second1 = compute(*second1)
    sum_x(*far0, x_far0)
    x_first1 = sum_near(*first1, y_first1)
    y_second1 = scatter_near(*second1, p_second1)
    z_0 = scatter_z(0)
    grad_tiles(0, 2)
    sum_x(*far1, x_far1)
    zg_0 = gather_z(0, z_0)
    grad_tiles(2, 4)
    x_second1 = sum_near(*second1, y_second1)
    sum_x(1, OWN, 1, 0, 2, x_first1)
    grad_tiles(4, 6)
    sum_x(1, OWN, 1, 2, 2, x_second1)
    xg_0 = gather_x(0, zg_0)
    z_1 = scatter_z(1)
    grad_tiles(6, 9)
    zg_1 = gather_z(1, z_1)
    grad_tiles(9, 12)
    xg_1 = gather_x(1, zg_1)
    wait_all(xg_0 + xg_1)
    for copy in sent:
        copy.wait_send()


N_SEND = 144


def local(out_grad, routes, gate_values, layer_input, w_gate, w_up, w_down):
    any_spec = pl.BlockSpec(memory_space=pl.ANY)
    vmem = pl.BlockSpec(memory_space=pltpu.VMEM)
    return pl.pallas_call(
        kernel,
        out_shape=(
            pltpu.VMEM((TOK, D), BF16),
            pltpu.VMEM((1, D, U), F32),
            pltpu.VMEM((1, D, U), F32),
        ),
        in_specs=[any_spec, vmem, vmem, any_spec, any_spec, any_spec, any_spec],
        out_specs=(vmem, vmem, vmem),
        scratch_shapes=[
            pltpu.VMEM((2, 2, 4, 2, HALF, D), BF16),
            pltpu.VMEM((D, 2 * U), BF16),
            pltpu.VMEM((2 * U, D), BF16),
            pltpu.VMEM((D, U), BF16),
            pltpu.VMEM((4, 2, EXPERTS, TOK), F32),
            pltpu.VMEM((2, 4, 2, HALF, 2 * U), BF16),
            pltpu.VMEM((2, 4, HALF, D), BF16),
            pltpu.VMEM((2, 4, HALF, D), BF16),
            pltpu.VMEM((2, 4, HALF, D), BF16),
            pltpu.VMEM((3, 2, 4, HALF, XCOLS), BF16),
            pltpu.VMEM((2, 4, HALF, XCOLS), BF16),
            pltpu.VMEM((NZ - 1, 2, ZROWS, ZCOLS), BF16),
            pltpu.VMEM((2, HALF, XCOLS), BF16),
            pltpu.VMEM((2, 3, HALF, XCOLS), BF16),
            pltpu.VMEM((2, HALF, D), BF16),
            pltpu.SemaphoreType.DMA((8,)),
            pltpu.SemaphoreType.DMA((N_SEND,)),
            pltpu.SemaphoreType.DMA((N_SEND,)),
        ],
        compiler_params=pltpu.CompilerParams(
            collective_id=0, has_side_effects=True, vmem_limit_bytes=56 * 2**20
        ),
        cost_estimate=pl.CostEstimate(
            flops=7 * 2 * 1024 * D * U, bytes_accessed=14 * 2**20, transcendentals=1024 * U
        ),
    )(out_grad, routes.T, gate_values.T, layer_input, w_gate, w_up, w_down)


def solution(mesh):
    placed = (
        P("expert", None),
        P("expert", None),
        P("expert", None),
        P("expert", None),
        P("expert", None, "dp"),
        P("expert", None, "dp"),
        P("expert", None, "dp"),
    )
    return jax.shard_map(
        local,
        mesh=mesh,
        in_specs=placed,
        out_specs=(P("expert", None), P("expert", None, "dp"), P("expert", None, "dp")),
        check_vma=False,
    )
```

time: 107 us -> 93.3 us (0.87)
  Pallas kernels: 101 us -> 88.4 us
    pallas_call x1, Pallas kernels: 101 us -> 88.4 us  [local(): pl.pallas_call(kernel, out_shape=(pltpu.VMEM((TOK, D), BF16), pltpu.VMEM(...]
where the time goes in v4:
time: 93.3 us; the launch traced here: 93.2 us
  Pallas kernels  88.4 us (95%)
  local copies, waits for them, and re-layouts  4.21 us (5%)
    pallas_call x1, Pallas kernels, local(): pl.pallas_call(kernel, out_shape=(pltpu.VMEM((TOK, D), BF16), pltpu.VMEM(...  88.4 us
    unnamed x3, local copies, waits for them, and re-layouts  4.21 us

profile of v4, /device:TPU:32, one launch (start us, length us, event | category | flops | bytes accessed | tf_op | source)
XLA Modules:
  0.0 93.2 jit_solution(389637076509466572)
XLA Ops:
  0.6 88.4 %shard_map.94 = (bf16[128,3072]{1,0:T(8,128)(2,1)S(1)}, f32[1,3072,256]{2,1,0:T(8,128)S(1)}, f32[1,3072,256]{2,1,0:T(8,128)S(1)}) custom-call(bf16[128,3072]{1,0:T(8,128)(2,1)} %og_in.1, s32[4,128]{1,0:T(4,128)} %bitcast.2, f32[4,128]{1,0:T(4,128)} %bitcast.3, bf16[128,3072]{1,0:T(8,128)(2,1)} %x_in.1, bf16[1,3072,256]{2,1,0:T(8,128)(2,1)} %wg_in.1, ...), custom_call_target="tpu_custom_call" | custom-call | flops 11274289152 | bytes 14680064 | tf_op jit(solution)/shard_map/pallas_call | solution.py:390
  89.0 0.9 copy.13
  89.9 1.7 %copy.14 = f32[1,3072,256]{2,1,0:T(8,128)} copy(f32[1,3072,256]{2,1,0:T(8,128)S(1)} %get-tuple-element.4) | data formatting | bytes 6291456
  91.6 1.7 %copy.15 = f32[1,3072,256]{2,1,0:T(8,128)} copy(f32[1,3072,256]{2,1,0:T(8,128)S(1)} %get-tuple-element.5) | data formatting | bytes 6291456

commit v5 on v4

--- a/solution.py
+++ b/solution.py
@@ -46,6 +46,11 @@
     to_x = {d: dev(x_at[d], y, z, c) for d in x_at}
     to_z = {d: dev(x, y, z_at[d], c) for d in z_at}
 
+    peers = [sib] + list(to_y.values()) + list(to_x.values()) + list(to_z.values())
+    barrier = pltpu.get_barrier_semaphore()
+    for device in peers:
+        pl.semaphore_signal(barrier, inc=1, device_id=device, device_id_type=MESH)
+
     loads = []
 
     def load(src, dst):
@@ -57,15 +62,19 @@
 
     sent = []
 
-    def send(src, dst, device):
+    def make(src, dst, device, condition=None):
         i = len(sent)
         assert i < N_SEND
         copy = pltpu.make_async_remote_copy(
             src_ref=src, dst_ref=dst, send_sem=send_sem.at[i], recv_sem=recv_sem.at[i],
             device_id=device, device_id_type=MESH,
         )
+        sent.append((copy, condition))
+        return copy
+
+    def send(src, dst, device):
+        copy = make(src, dst, device)
         copy.start()
-        sent.append(copy)
         return copy
 
     own_loads = {}
@@ -78,11 +87,6 @@
         load(wd_in.at[0], wd),
     ]
 
-    peers = [sib] + list(to_y.values()) + list(to_x.values()) + list(to_z.values())
-    barrier = pltpu.get_barrier_semaphore()
-    for device in peers:
-        pl.semaphore_signal(barrier, inc=1, device_id=device, device_id_type=MESH)
-
     lane = lax.broadcasted_iota(jnp.int32, (TOK, TOK), 1)
     row = lax.broadcasted_iota(jnp.int32, (TOK, TOK), 0)
     for e in range(EXPERTS):
@@ -91,9 +95,9 @@
         )
 
     pl.semaphore_wait(barrier, len(peers))
-
     g_move = {j: send(g8.at[OWN, 0], g8.at[j, 0], to_y[d]) for j, d in TO_Y}
     g_swap = {OWN: send(g8.at[OWN, 0], g8.at[OWN, 1], sib)}
+
     x_cols = pl.ds(pl.multiple_of(x * XCOLS, XCOLS), XCOLS)
     z_cols = pl.ds(pl.multiple_of(z * FAR_COLS, FAR_COLS), FAR_COLS)
 
@@ -269,7 +273,7 @@
     def scatter_z(h):
         wait_all(y_got[h])
         total = u[h, OWN].astype(F32)
-        for j in range(3) if h == 0 else (FAR - 1,):
+        for j in range(3):
             total = total + yr[h, j].astype(F32)
         v[h] = total.astype(BF16)
         got = []
@@ -289,6 +293,49 @@
         out[rows, cols] = total.astype(BF16)
         piece = out.at[rows, cols]
         return [send(piece, piece, to_z[d]) for d in Z_ORDER]
+
+    def owns(nz, part):
+        return lax.div(lax.rem(nz, 4), 2) == part
+
+    def scatter_z_part(part):
+        if part == 0:
+            wait_all(y_got[1])
+        sub = groups(2 * part, 2)
+        v[1, sub] = (u[1, OWN, sub].astype(F32) + yr[1, FAR - 1, sub].astype(F32)).astype(BF16)
+        got = []
+        for d in Z_ORDER:
+            rows, cols = z_part(z_at[d])
+            theirs = owns(z_at[d], part)
+            copy = make(v.at[1, rows, cols], zr.at[d - 1, 1], to_z[d], theirs)
+            pl.when(theirs)(copy.start)
+            got.append(copy)
+        return got
+
+    def gather_z_part(part, got):
+        rows, cols = z_part(z)
+        out_rows = pl.ds(pl.multiple_of(HALF + lax.rem(z, 4) * ZROWS, ZROWS), ZROWS)
+        out_cols = pl.ds(pl.multiple_of(x * XCOLS + lax.div(z, 4) * ZCOLS, ZCOLS), ZCOLS)
+        piece = out.at[out_rows, out_cols]
+        mine = owns(z, part)
+        gathered = [(d, make(piece, piece, to_z[d], mine)) for d in Z_ORDER]
+
+        @pl.when(mine)
+        def _():
+            wait_all(got)
+            total = v[1, rows, cols].astype(F32)
+            for d in range(NZ - 1):
+                total = total + zr[d, 1].astype(F32)
+            out[out_rows, out_cols] = total.astype(BF16)
+            for _, copy in gathered:
+                copy.start()
+
+        return gathered
+
+    def gather_x_part(part, gathered):
+        for d, copy in gathered:
+            pl.when(owns(lax.rem(z + NZ - d, NZ), part))(copy.wait_recv)
+        piece = out.at[pl.ds(HALF + part * 2 * ZROWS, 2 * ZROWS), x_cols]
+        return [send(piece, piece, to_x[d]) for d in X_ORDER]
 
     def gather_x(h, got):
         wait_all(got)
@@ -327,6 +374,7 @@
     p_own0 = compute(*own0)
     far_0, shared_0 = share(0, small_0)
     far_1, shared_1 = share(1, small_1)
+    first_1 = send_direct(1, 0, 2)
     p_own1 = compute(*own1)
     for j, _ in TO_Y:
         g_move[j].wait_recv()
@@ -334,7 +382,6 @@
     x_own0 = scatter_x(*own0, p_own0)
     merge(*own1, p_own1)
     near_arrive(0, first_0, 0, 2)
-    first_1 = send_direct(1, 0, 2)
     near_arrive(0, second_0, 2, 2 - NEAR_X)
     second_1 = send_direct(1, 2, 2 - NEAR_X)
     if NEAR_X:
@@ -361,27 +408,32 @@
     sum_x(*far0, x_far0)
     x_first1 = sum_near(*first1, y_first1)
     y_second1 = scatter_near(*second1, p_second1)
+    grad_tiles(0, 4)
     z_0 = scatter_z(0)
-    grad_tiles(0, 2)
     sum_x(*far1, x_far1)
     zg_0 = gather_z(0, z_0)
-    grad_tiles(2, 4)
+    sum_x(1, OWN, 1, 0, 2, x_first1)
     x_second1 = sum_near(*second1, y_second1)
-    sum_x(1, OWN, 1, 0, 2, x_first1)
-    grad_tiles(4, 6)
+    z_first = scatter_z_part(0)
+    grad_tiles(4, 8)
+    zg_first = gather_z_part(0, z_first)
     sum_x(1, OWN, 1, 2, 2, x_second1)
+    z_second = scatter_z_part(1)
     xg_0 = gather_x(0, zg_0)
-    z_1 = scatter_z(1)
-    grad_tiles(6, 9)
-    zg_1 = gather_z(1, z_1)
-    grad_tiles(9, 12)
-    xg_1 = gather_x(1, zg_1)
-    wait_all(xg_0 + xg_1)
-    for copy in sent:
-        copy.wait_send()
-
-
-N_SEND = 144
+    grad_tiles(8, 10)
+    xg_first = gather_x_part(0, zg_first)
+    zg_second = gather_z_part(1, z_second)
+    grad_tiles(10, 12)
+    xg_second = gather_x_part(1, zg_second)
+    wait_all(xg_0 + xg_first + xg_second)
+    for copy, condition in sent:
+        if condition is None:
+            copy.wait_send()
+        else:
+            pl.when(condition)(copy.wait_send)
+
+
+N_SEND = 160
 
 
 def local(out_grad, routes, gate_values, layer_input, w_gate, w_up, w_down):

time: 93.3 us -> 93.4 us (level)
  no operation moved by 1% of the time
where the time goes in v5:
time: 93.4 us; the launch traced here: 93.3 us
  Pallas kernels  88.4 us (95%)
  local copies, waits for them, and re-layouts  4.21 us (5%)
    pallas_call x1, Pallas kernels, local(): pl.pallas_call(kernel, out_shape=(pltpu.VMEM((TOK, D), BF16), pltpu.VMEM(...  88.4 us
    unnamed x3, local copies, waits for them, and re-layouts  4.21 us

profile of v5, /device:TPU:32, one launch (start us, length us, event | category | flops | bytes accessed | tf_op | source)
XLA Modules:
  0.0 93.3 jit_solution(3898361053447057906)
XLA Ops:
  0.6 88.4 %shard_map.94 = (bf16[128,3072]{1,0:T(8,128)(2,1)S(1)}, f32[1,3072,256]{2,1,0:T(8,128)S(1)}, f32[1,3072,256]{2,1,0:T(8,128)S(1)}) custom-call(bf16[128,3072]{1,0:T(8,128)(2,1)} %og_in.1, s32[4,128]{1,0:T(4,128)} %bitcast.2, f32[4,128]{1,0:T(4,128)} %bitcast.3, bf16[128,3072]{1,0:T(8,128)(2,1)} %x_in.1, bf16[1,3072,256]{2,1,0:T(8,128)(2,1)} %wg_in.1, ...), custom_call_target="tpu_custom_call" | custom-call | flops 11274289152 | bytes 14680064 | tf_op jit(solution)/shard_map/pallas_call | solution.py:442
  89.0 0.9 copy.13
  89.9 1.7 %copy.14 = f32[1,3072,256]{2,1,0:T(8,128)} copy(f32[1,3072,256]{2,1,0:T(8,128)S(1)} %get-tuple-element.4) | data formatting | bytes 6291456
  91.6 1.7 %copy.15 = f32[1,3072,256]{2,1,0:T(8,128)} copy(f32[1,3072,256]{2,1,0:T(8,128)S(1)} %get-tuple-element.5) | data formatting | bytes 6291456

commit v6 on v5

--- a/solution.py
+++ b/solution.py
@@ -205,21 +205,20 @@
         both = jnp.concatenate([gate_grad, up_grad], axis=1)
         dg[h, j : j + n, :, sub] = both.reshape(n, 2, count * 16, 2 * U)
 
-        def tile(i, carry):
-            cols = pl.ds(pl.multiple_of(i * BACK, BACK), BACK)
+        sends = []
+        for i in range(D // BACK):
+            cols = pl.ds(i * BACK, BACK)
             part = jnp.dot(both, wgu_t[:, cols], preferred_element_type=F32)
             part = part.astype(BF16).reshape(n, 2, count * 16, BACK)
+            ps[h, j : j + n, sub, cols] = part[:, 1]
+            piece = (h, pl.ds(j, n), sub, cols)
+            sends.append(send(ps.at[piece], pr.at[piece], sib))
             s[h, j : j + n, sub, cols] = part[:, 0]
-            ps[h, j : j + n, sub, cols] = part[:, 1]
-            return carry
-
-        lax.fori_loop(0, D // BACK, tile, 0)
-        piece = (h, pl.ds(j, n), sub)
-        return send(ps.at[piece], pr.at[piece], sib)
+        return sends
 
     def merge(h, j, n, first, count, parts):
         sub = groups(first, count)
-        parts.wait_recv()
+        wait_all(parts)
         for jj in range(j, j + n):
             s[h, jj, sub] = (s[h, jj, sub].astype(F32) + pr[h, jj, sub].astype(F32)).astype(BF16)
 
@@ -433,7 +432,7 @@
             pl.when(condition)(copy.wait_send)
 
 
-N_SEND = 160
+N_SEND = 176
 
 
 def local(out_grad, routes, gate_values, layer_input, w_gate, w_up, w_down):

time: 93.4 us -> 94.6 us (1.013)
  Pallas kernels: 88.4 us -> 89.6 us
    pallas_call x1, Pallas kernels: 88.4 us -> 89.6 us  [local(): pl.pallas_call(kernel, out_shape=(pltpu.VMEM((TOK, D), BF16), pltpu.VMEM(...]
where the time goes in v6:
time: 94.6 us; the launch traced here: 94.4 us
  Pallas kernels  89.6 us (95%)
  local copies, waits for them, and re-layouts  4.21 us (4%)
    pallas_call x1, Pallas kernels, local(): pl.pallas_call(kernel, out_shape=(pltpu.VMEM((TOK, D), BF16), pltpu.VMEM(...  89.6 us
    unnamed x3, local copies, waits for them, and re-layouts  4.21 us

profile of v6, /device:TPU:32, one launch (start us, length us, event | category | flops | bytes accessed | tf_op | source)
XLA Modules:
  0.0 94.4 jit_solution(13936293066934586211)
XLA Ops:
  0.6 89.6 %shard_map.94 = (bf16[128,3072]{1,0:T(8,128)(2,1)S(1)}, f32[1,3072,256]{2,1,0:T(8,128)S(1)}, f32[1,3072,256]{2,1,0:T(8,128)S(1)}) custom-call(bf16[128,3072]{1,0:T(8,128)(2,1)} %og_in.1, s32[4,128]{1,0:T(4,128)} %bitcast.2, f32[4,128]{1,0:T(4,128)} %bitcast.3, bf16[128,3072]{1,0:T(8,128)(2,1)} %x_in.1, bf16[1,3072,256]{2,1,0:T(8,128)(2,1)} %wg_in.1, ...), custom_call_target="tpu_custom_call" | custom-call | flops 11274289152 | bytes 14680064 | tf_op jit(solution)/shard_map/pallas_call | solution.py:441
  90.2 0.9 copy.13
  91.1 1.7 %copy.14 = f32[1,3072,256]{2,1,0:T(8,128)} copy(f32[1,3072,256]{2,1,0:T(8,128)S(1)} %get-tuple-element.4) | data formatting | bytes 6291456
  92.8 1.7 %copy.15 = f32[1,3072,256]{2,1,0:T(8,128)} copy(f32[1,3072,256]{2,1,0:T(8,128)S(1)} %get-tuple-element.5) | data formatting | bytes 6291456
